TPU v7x, 256 devices: a whole 4x4x8 slice. The times are simulated.
256 devices in a mesh: sx: 8 (over y, core), sy: 32 (over x, z).
Axes of the slice: x: 4, y: 4, z: 8, core: 2. Of those that a mesh axis runs over, the one named last changes fastest.
Arguments:
- residual: float32 [96, 331776], P(None, ('sx', 'sy')), may hold values from -52 to 52
- ritz_block: float32 [96, 331776], P(None, ('sx', 'sy')), may hold values from -52 to 52
- search_block: float32 [96, 331776], P(None, ('sx', 'sy')), may hold values from -52 to 52
- inverse_factor: float32 [8, 32, 1600, 1600], P('sx', 'sy'), may hold values from -2.5 to 2.5, as said below
- send_rows: int32 [8, 32, 8, 128], P('sx', 'sy'), may hold values from 0 to 1295
- send_count: int32 [8, 32, 8], P('sx', 'sy'), may hold values from 0 to 72, as said below
Outputs:
- precond: float32 [96, 331776], P(None, ('sx', 'sy'))
- gram: float32 [288, 288], replicated
Inputs may be any that keep to these rules, and one draw needn't show every extreme that they name: `send_rows`: entries from send_count on are padding, read by nothing. `send_count`: directions 0 to 3 carry 36 to 72 vertices, directions 4 to 7 one to 4; both bounds are reached in every draw; zero exactly where the neighbour lies outside the grid. `inverse_factor`: lower triangular, diagonal from 0.5 to 2.
All inputs are finite; a program needn't handle non-finite values.
Results may differ from a plain program's by a relative error of at most 0.00055.
Values sent between devices are 32-bit elements; how exact they have to be, the bound alone decides.
No kernel may reach another device: no remote copies, remote signals or barrier semaphores. Data moves between devices by JAX's collectives and lax.ppermute only.
A program may use at most 64 MiB of HBM per device.

v0:
```python
import jax
import jax.numpy as jnp
from jax import lax
from jax.experimental import pallas as pl
from jax.experimental.pallas import tpu as pltpu
from jax.sharding import PartitionSpec as P

EDGE = 72
LANES = 128
TAIL = 1280
F32 = jnp.float32
BF16 = jnp.bfloat16
VMEM = pl.BlockSpec(memory_space=pltpu.VMEM)
HBM = pl.BlockSpec(memory_space=pl.ANY)
NN = (((1,), (0,)), ((), ()))
NT = (((1,), (1,)), ((), ()))


def split(value):
    high = value.astype(BF16)
    low = (value - high.astype(F32)).astype(BF16)
    return high, low


def dot(left, right, dims):
    return lax.dot_general(left, right, dims, preferred_element_type=F32)


def dot_pairs(left, right, dims):
    rows = left[0].shape[0]
    both = dot(jnp.concatenate(left, axis=0), right[0], dims)
    return both[:rows] + both[rows:] + dot(left[0], right[1], dims)


def dot_exact(left, right, dims):
    rows = left[0].shape[0]
    both = dot(jnp.concatenate(left, axis=0), right, dims)
    return both[:rows] + both[rows:]


def pick(flag, when_even, when_odd):
    return jnp.where(flag[:, : when_even.shape[1]] == 0, when_even, when_odd)


def call(kernel, out, in_specs, scratch=(), flops=0, moved=0, name=None, out_specs=None, limit=20):
    return pl.pallas_call(
        kernel,
        out_shape=out,
        in_specs=in_specs,
        out_specs=jax.tree.map(lambda _: VMEM, out) if out_specs is None else out_specs,
        scratch_shapes=list(scratch),
        compiler_params=pltpu.CompilerParams(vmem_limit_bytes=limit * 1024 * 1024),
        cost_estimate=pl.CostEstimate(flops=flops, bytes_accessed=moved, transcendentals=0),
        name=name,
    )


def shaped(*shape, dtype=F32):
    return jax.ShapeDtypeStruct(shape, dtype)


def in_hbm(value):
    return pltpu.with_memory_space_constraint(value, pltpu.HBM)


def gather_kernel(
    odd, count_hbm, rows_hbm, res_hbm, factor, sxa, sxb, sya, syb, field, ids, slab, count, rows, res, sem
):
    fetch_count = pltpu.make_async_copy(count_hbm, count, sem.at[0])
    fetch_rows = pltpu.make_async_copy(rows_hbm, rows, sem.at[1])
    fetch_res = pltpu.make_async_copy(res_hbm, res, sem.at[2])
    fetch_count.start()
    fetch_rows.start()
    fetch_res.start()
    fetch_slab = pltpu.make_async_copy(factor.at[0, 0, pl.ds(TAIL, 320), :], slab, sem.at[3])
    fetch_slab.start()
    lane = lax.broadcasted_iota(jnp.int32, (1, LANES), 1)
    fetch_count.wait()
    fetch_rows.wait()
    table = rows[0, 0]

    def live(n):
        return count[0, 0, n]

    def edge(n):
        return jnp.where(lane < live(n), table[n : n + 1], -1)

    def corner(base, n, at):
        moved = pltpu.roll(table, at, 1)[n : n + 1]
        return jnp.where((lane >= at) & (lane < at + live(n)), moved, base)

    down = corner(corner(edge(0), 4, 72), 5, 80)
    up = corner(corner(edge(1), 6, 76), 7, 84)
    right, left = edge(2), edge(3)
    lists = [
        pick(odd[0:1], down, up),
        pick(odd[0:1], up, down),
        pick(odd[1:2], right, left),
        pick(odd[1:2], left, right),
    ]
    for k, values in enumerate(lists + lists):
        ids[k : k + 1] = values
    own = res.shape[1]
    row = lax.broadcasted_iota(jnp.int32, (own, LANES), 0)
    ones = [jnp.where(row == values, 1.0, 0.0).astype(BF16) for values in lists]
    onehot = jnp.concatenate(ones, axis=1)
    fetch_res.wait()
    high, low = split(res[...])
    field[:96] = high
    field[96:] = low
    packed = dot(field[...], onehot, NN)
    packed = packed[:96] + packed[96:]
    for k, out in enumerate((sxa, sxb, sya, syb)):
        out[...] = packed[:, k * LANES : (k + 1) * LANES]
    fetch_slab.wait()


def halo_place():
    col = lax.broadcasted_iota(jnp.int32, (320, 4 * LANES), 0) - 16
    spot = lax.broadcasted_iota(jnp.int32, (1, 4 * LANES), 1)
    lane = spot % LANES
    block = spot // LANES
    source = jnp.where(lane < EDGE, block * EDGE + lane, -99)
    for n, b, at in ((4, 2, 72), (6, 2, 76), (5, 3, 80), (7, 3, 84)):
        inside = (block == b) & (lane >= at) & (lane < at + 4)
        source = jnp.where(inside, 4 * EDGE + (n - 4) * 4 + lane - at, source)
    return jnp.where(col == source, 1.0, 0.0).astype(BF16)


def fetch(pairs, sem):
    copies = [pltpu.make_async_copy(source, dest, sem.at[k]) for k, (source, dest) in enumerate(pairs)]
    for copy in copies:
        copy.start()
    return copies


def own_slab(factor, k):
    return factor.at[0, 0, pl.ds(256 * k, 256), pl.ds(0, 256 * (k + 1))]


def tail_kernel(
    field, slab, factor, ritz_hbm, search_hbm, part, ph, plo, th, tlo, oh, olo, ritz, search, slab0, slab1, slab2, sem
):
    slabs = [(own_slab(factor, k), dest) for k, dest in enumerate((slab0, slab1, slab2))]
    copies = fetch([(ritz_hbm, ritz), (search_hbm, search)] + slabs, sem)
    place = halo_place()
    own = field.shape[1]
    oh[...], olo[...] = split(slab[:, :own])
    part[...] = dot_pairs((field[:96], field[96:]), (oh[...], olo[...]), NT)
    for value, out, turned in zip(split(slab[:, TAIL:]), (ph, plo), (th, tlo)):
        placed = dot(value, place, NN)
        out[...] = placed.astype(BF16)
        turned[...] = placed.T.astype(BF16)
    for copy in copies:
        copy.wait()


def halo_kernel(odd, sxa, sxb, sya, syb, part, ph, plo, th, tlo, given, half, bxa, bxb, bya, byb):
    xa, xb, ya, yb = sxa[...], sxb[...], sya[...], syb[...]
    arrived = jnp.concatenate(
        [pick(odd[0:1], xb, xa), pick(odd[0:1], xa, xb), pick(odd[1:2], yb, ya), pick(odd[1:2], ya, yb)], axis=1
    )
    solved = part[...] + dot_pairs(split(arrived), (th[...], tlo[...]), NN)
    half[...] = solved
    back = dot_pairs(split(solved), (ph[...], plo[...]), NN)
    b = [back[:, k * LANES : (k + 1) * LANES] for k in range(4)]
    bxa[...] = pick(odd[0:1], b[1], b[0])
    bxb[...] = pick(odd[0:1], b[0], b[1])
    bya[:96] = pick(odd[1:2], b[3], b[2])
    bya[96:] = given[...]
    byb[...] = pick(odd[1:2], b[2], b[3])


def slab_term(field, slab):
    width = slab.shape[1]
    block = split(slab[...])
    solved = dot_pairs((field[:96, :width], field[96:, :width]), block, NT)
    return dot_pairs(split(solved), block, NN)


def head_kernel(field, slab0, slab1, out):
    out[...] = slab_term(field, slab1)
    out[:, :256] = out[:, :256] + slab_term(field, slab0)


def last_kernel(field, slab2, slab3, head, factor, out, slab4, sem):
    (copy,) = fetch([(own_slab(factor, 4), slab4)], sem)
    out[:, :1024] = slab_term(field, slab3)
    out[:, :768] = out[:, :768] + slab_term(field, slab2)
    out[:, :512] = out[:, :512] + head[...]
    copy.wait()
    term = slab_term(field, slab4)
    out[:, :1024] = out[:, :1024] + term[:, :1024]
    out[:, 1024:] = term[:, 1024:]


def distinct_tiles(square):
    tiles = [square[32 * i : 32 * i + 32, 32 * j : 32 * j + 32] for i in range(3) for j in range(i, 3)]
    return jnp.concatenate(tiles, axis=0)


def whole_square(tiles):
    t = [tiles[32 * k : 32 * k + 32] for k in range(6)]
    blank = jnp.zeros((32, 32), F32)
    upper = jnp.concatenate(
        [
            jnp.concatenate([t[0], t[1], t[2]], axis=1),
            jnp.concatenate([blank, t[3], t[4]], axis=1),
            jnp.concatenate([blank, blank, t[5]], axis=1),
        ],
        axis=0,
    )
    row = lax.broadcasted_iota(jnp.int32, (96, 96), 0) // 32
    col = lax.broadcasted_iota(jnp.int32, (96, 96), 1) // 32
    return jnp.where(row <= col, upper, upper.T)


def side_kernel(
    odd, ids, ritz, search, factor, held, given, turned, same, sides_h, sides_l, rgh, rgl, slab3, sem
):
    copies = fetch([(own_slab(factor, 3), slab3)], sem)
    own = ritz.shape[1]
    numbers = ids[...].astype(F32)
    columns = numbers.T
    live = jnp.where(columns < 0.0, -2.0, columns)
    across = lax.broadcasted_iota(jnp.int32, (LANES, own), 1).astype(F32)
    for k in range(4):
        lanes = slice(k * LANES, (k + 1) * LANES)
        turned[lanes] = jnp.where(columns[:, k : k + 1] == across, 1.0, 0.0).astype(BF16)
        for j in range(4):
            agree = live[:, k : k + 1] == numbers[j : j + 1]
            same[lanes, j * LANES : (j + 1) * LANES] = jnp.where(agree, 1.0, 0.0).astype(BF16)
    blank = jnp.zeros((32, own), BF16)
    for r, s, out in zip(split(ritz[...]), split(search[...]), (sides_h, sides_l)):
        out[:96] = r
        out[96:128] = blank
        out[128:224] = s
        out[224:] = blank
    for side, out in zip((sides_h, sides_l), (rgh, rgl)):
        out[...] = dot(turned[...], side[...], NT).astype(BF16)
    pair = (sides_h[...], sides_l[...])
    cross = dot_pairs(pair, pair, NT)
    rr, sr, ss = cross[:96, :96], cross[128:224, :96], cross[128:224, LANES : LANES + 96]
    rt, st = distinct_tiles(rr), distinct_tiles(ss)
    first = jnp.concatenate([sr, rt[:96]], axis=1)
    second = jnp.concatenate([rt[96:], st[:96], st[96:], jnp.zeros((96, 32), F32)], axis=1)
    held[...] = pick(odd[1:2], first, second)
    given[...] = pick(odd[1:2], second, first)
    for copy in copies:
        copy.wait()


def local_kernel(own_part, half, oh, olo, turned, sides_h, sides_l, local, sent, base):
    add = dot_pairs(split(half[...]), (oh[...], olo[...]), NN)
    value = add + jnp.concatenate([own_part[...], jnp.zeros((96, add.shape[1] - TAIL), F32)], axis=1)
    local[...] = value
    pair = split(value)
    sent[...] = dot_exact(pair, turned[...], NT)
    base[:96] = dot_pairs(pair, pair, NT)
    cross = dot_pairs(pair, (sides_h[...], sides_l[...]), NT)
    base[96:192] = cross[:, :96]
    base[192:] = cross[:, LANES : LANES + 96]


def gram_kernel(odd, rxa, rxb, rya, ryb, same, sent, rgh, rgl, base, held, away, kept, back):
    back[...] = jnp.concatenate([rxa[...], rxb[...], rya[:96], ryb[...]], axis=1)
    pair = split(back[...])
    mixed = sent[...] + 0.5 * dot_exact(pair, same[...], NN)
    square = dot_pairs(split(mixed), pair, NT)
    cross = dot_pairs(pair, (rgh[...], rgl[...]), NN)
    pp = base[:96] + square + square.T
    pr = base[96:192] + cross[:, :96]
    ps = base[192:] + cross[:, LANES : LANES + 96]
    tiles = distinct_tiles(pp)
    first = jnp.concatenate([pr, tiles[:96]], axis=1)
    second = jnp.concatenate([ps, tiles[96:]], axis=1)
    kept[:96] = pick(odd[0:1], first, second)
    away[:96] = pick(odd[0:1], second, first)
    early = held[...] + rya[96:]
    kept[96:] = pick(odd[0:1], early[:48], early[48:])
    away[96:] = pick(odd[0:1], early[48:], early[:48])


def update_kernel(back, turned, local, precond):
    precond[...] = local[...] + dot_exact(split(back[...]), turned[...], NN)


def final_kernel(scale, odd, mine, other, gram, out, sem):
    def by_core(rows):
        a, b = mine[rows], other[rows]
        return pick(odd[0:1], a, b) * scale, pick(odd[0:1], b, a) * scale

    late = by_core(slice(0, 96))
    near, far = by_core(slice(96, 144)), by_core(slice(144, 192))
    near, far = jnp.concatenate(near, axis=0), jnp.concatenate(far, axis=0)
    first, second = pick(odd[1:2], near, far), pick(odd[1:2], far, near)
    pr, ps = late[0][:, :96], late[1][:, :96]
    pp = whole_square(jnp.concatenate([late[0][:, 96:], late[1][:, 96:]], axis=0))
    sr = first[:, :96]
    rr = whole_square(jnp.concatenate([first[:, 96:], second[:, :32]], axis=0))
    ss = whole_square(jnp.concatenate([second[:, 32:64], second[:, 64:96]], axis=0))
    copies = []
    bands = ([pr, pp, ps], [rr, pr.T, sr.T], [sr, ps.T, ss])
    for k, parts in zip((1, 0, 2), bands):
        rows = slice(96 * k, 96 * (k + 1))
        out[rows] = jnp.concatenate(parts, axis=1)
        copies.append(pltpu.make_async_copy(out.at[rows], gram.at[rows], sem.at[k]))
        copies[-1].start()
    for copy in copies:
        copy.wait()


def swap(block, axis, step):
    return lax.ppermute(block, axis, [(i, i ^ step) for i in range(lax.axis_size(axis))])


def swap_odd(block, axis):
    size = lax.axis_size(axis)
    route = [(i, (i + 1) % size) for i in range(1, size, 2)]
    return lax.ppermute(block, axis, route + [(b, a) for a, b in route])


def body(residual, ritz_block, search_block, inverse_factor, send_rows, send_count):
    own = residual.shape[1]
    p, q = lax.axis_index("sx"), lax.axis_index("sy")
    odd = jnp.where(jnp.arange(8)[:, None] == 0, p % 2, q % 2) + jnp.zeros((8, LANES), jnp.int32)
    lane = jnp.arange(LANES)[None, :]
    msg = shaped(96, LANES)

    factor = in_hbm(inverse_factor)
    sxa, sxb, sya, syb, field, ids, slab = call(
        gather_kernel,
        (
            msg,
            msg,
            msg,
            msg,
            shaped(192, own, dtype=BF16),
            shaped(8, LANES, dtype=jnp.int32),
            shaped(320, 1600),
        ),
        [VMEM, HBM, HBM, HBM, HBM],
        [
            pltpu.SMEM((1, 1, 8), jnp.int32),
            pltpu.VMEM((1, 1, 8, LANES), jnp.int32),
            pltpu.VMEM((96, own), F32),
            pltpu.SemaphoreType.DMA((4,)),
        ],
        flops=2 * 192 * 1296 * 512,
        moved=2000000,
        name="gather",
    )(odd, in_hbm(send_count), in_hbm(send_rows), in_hbm(residual), factor)

    gxb, gxa = swap_odd(sxb, "sx"), swap(sxa, "sx", 1)

    placed, turned = shaped(320, 512, dtype=BF16), shaped(512, 320, dtype=BF16)
    wide = shaped(320, own, dtype=BF16)
    part, ph, plo, th, tlo, oh, olo, ritz, search, slab0, slab1, slab2 = call(
        tail_kernel,
        (shaped(96, 320), placed, placed, turned, turned, wide, wide)
        + (shaped(96, own), shaped(96, own), shaped(256, 256), shaped(256, 512), shaped(256, 768)),
        [VMEM, VMEM, HBM, HBM, HBM],
        [pltpu.SemaphoreType.DMA((5,))],
        flops=2 * 96 * 1296 * 320 * 3,
        moved=6000000,
        name="tail",
    )(field, slab, factor, in_hbm(ritz_block), in_hbm(search_block))
    gxa, gxb, part = lax.optimization_barrier((gxa, gxb, part))

    relay = jnp.where(lane >= EDGE, gxa + gxb, 0.0)
    gyb, gya = swap_odd(syb + relay, "sy"), swap(sya + relay, "sy", 1)

    sides, sent_sides = shaped(2 * LANES, own, dtype=BF16), shaped(512, 2 * LANES, dtype=BF16)
    held, given, turned, same, sides_h, sides_l, rgh, rgl, slab3 = call(
        side_kernel,
        (
            msg,
            msg,
            shaped(512, own, dtype=BF16),
            shaped(512, 512, dtype=BF16),
            sides,
            sides,
            sent_sides,
            sent_sides,
            shaped(256, 1024),
        ),
        [VMEM] + [VMEM] * 3 + [HBM],
        [pltpu.SemaphoreType.DMA((1,))],
        flops=2 * 192 * 256 * 1296 * 3,
        moved=3000000,
        name="side",
    )(odd, ids, ritz, search, factor)

    head = call(
        head_kernel,
        shaped(96, 512),
        [VMEM] * 3,
        flops=2 * 2 * 96 * 256 * 256 * 3 * 3,
        moved=1200000,
        name="head",
    )(field, slab0, slab1)
    gya, gyb, head = lax.optimization_barrier((gya, gyb, head))

    half, bxa, bxb, bya, byb = call(
        halo_kernel,
        (shaped(96, 320), msg, msg, shaped(192, LANES), msg),
        [VMEM] + [VMEM] * 10,
        flops=2 * 2 * 96 * 320 * 512 * 3,
        moved=1000000,
        name="halo",
    )(odd, gxa, gxb, gya, gyb, part, ph, plo, th, tlo, given)

    ryb, rya = swap_odd(byb, "sy"), swap(bya, "sy", 1)

    own_part = call(
        last_kernel,
        shaped(96, TAIL),
        [VMEM] * 4 + [HBM],
        [pltpu.VMEM((256, TAIL), F32), pltpu.SemaphoreType.DMA((1,))],
        flops=2 * 2 * 96 * 256 * 256 * 12 * 3,
        moved=3000000,
        name="last",
    )(field, slab2, slab3, head, factor)
    rya, ryb, own_part = lax.optimization_barrier((rya, ryb, own_part))

    relay = jnp.where(lane >= EDGE, rya[:96] + ryb, 0.0)
    rxb, rxa = swap_odd(bxb + relay, "sx"), swap(bxa + relay, "sx", 1)

    local, sent, base = call(
        local_kernel,
        (shaped(96, own), shaped(96, 512), shaped(288, 96)),
        [VMEM] * 7,
        flops=2 * 96 * 1296 * 1100 * 3,
        moved=4000000,
        name="local",
    )(own_part, half, oh, olo, turned, sides_h, sides_l)

    away, kept, back = call(
        gram_kernel,
        (shaped(144, LANES), shaped(144, LANES), shaped(96, 512)),
        [VMEM] + [VMEM] * 10,
        flops=2 * 96 * 512 * 900 * 3,
        moved=2000000,
        name="gram",
    )(odd, rxa, rxb, rya, ryb, same, sent, rgh, rgl, base, held)

    precond = call(
        update_kernel,
        shaped(96, own),
        [VMEM] * 3,
        flops=2 * 192 * 1296 * 512,
        moved=3000000,
        name="update",
    )(back, turned, local)

    def summed(value, axis, steps):
        total = swap(value, axis, steps[0])
        for step in steps[1:]:
            total = total + swap(value, axis, step)
        return value + total

    def summed_apart(value, first):
        rows, cols = lax.axis_size("sx"), lax.axis_size("sy")

        def partner(r, c, step):
            return (r ^ (2 * step), c) if r % 2 == first else (r, c ^ (8 * step))

        def moved(step):
            route = []
            for r in range(rows):
                for c in range(cols):
                    to_row, to_col = partner(r, c, step)
                    route.append((r * cols + c, to_row * cols + to_col))
            return lax.ppermute(value, ("sx", "sy"), route)

        total = moved(1)
        for step in (3, 2):
            total = total + moved(step)
        return value + total

    total = kept + swap(away, "sx", 1)
    total = summed_apart(total, 0)
    total = summed_apart(total, 1)
    total = summed(total, "sy", (6,))
    total, precond = lax.optimization_barrier((total, precond))
    three, two, one = (swap(total, "sy", step) for step in (3, 2, 1))
    late = (total[:96] + one[:96]) + (two[:96] + three[:96])
    mine = jnp.concatenate([late, total[96:] + two[96:], one[96:] + three[96:]], axis=0)
    other = swap(mine, "sx", 1)

    vertex_total = own * lax.axis_size("sx") * lax.axis_size("sy")

    def finish(odd, *refs):
        final_kernel(1.0 / vertex_total, odd, *refs)

    gram = call(
        finish,
        shaped(288, 288),
        [VMEM] * 3,
        [pltpu.VMEM((288, 288), F32), pltpu.SemaphoreType.DMA((3,))],
        flops=1000000,
        moved=700000,
        name="final",
        out_specs=HBM,
    )(odd, mine, other)
    return precond, gram


def solution(mesh):
    placed = (
        P(None, ("sx", "sy")),
        P(None, ("sx", "sy")),
        P(None, ("sx", "sy")),
        P("sx", "sy", None, None),
        P("sx", "sy", None, None),
        P("sx", "sy", None),
    )
    return jax.shard_map(
        body, mesh=mesh, in_specs=placed, out_specs=(P(None, ("sx", "sy")), P()), check_vma=False
    )
```

profile of v0, /device:TPU:1, one launch (start us, length us, event | category | flops | bytes accessed | tf_op | source)
XLA Modules:
  0.0 67.4 jit_solution(58438466596908338)
XLA Ops:
  0.7 0.1 add.71.odd
  0.7 1.8 %gather.1 = (f32[96,128]{1,0:T(8,128)S(1)}, f32[96,128]{1,0:T(8,128)S(1)}, f32[96,128]{1,0:T(8,128)S(1)}, f32[96,128]{1,0:T(8,128)S(1)}, bf16[192,1296]{1,0:T(8,...) custom-call(s32[8,128]{1,0:T(8,128)S(1)} %add.71.odd, s32[1,1,8]{2,1,0:T(1,128)} %count_hbm.1, ...), custom_call_target="tpu_custom_call" | custom-call | flops 254803968 | bytes 2000000 | tf_op jit(solution)/shard_map/gather/pallas_call | solution.py:331
  2.6 3.3 %collective-permute-start = (f32[96,128]{1,0:T(8,128)S(1)}, f32[96,128]{1,0:T(8,128)S(1)}, u32[]{:S(2)}, u32[]{:S(2)}) collective-permute-start(f32[96,128]{1,0:T(8,128)S(1)} %get-tuple-element.52), channel_id=1, source_target_pairs={{0,32},{32,0},{64,96},{96,64},{128,160},{160,128},{192,224},{224,1... | collective-permute-start | bytes 147464 | tf_op jit(solution)/shard_map/ppermute | solution.py:314
  5.9 0.0 collective-permute-start.1
  5.9 2.8 %tail.1 = (f32[96,320]{1,0:T(8,128)S(1)}, bf16[320,512]{1,0:T(8,128)(2,1)S(1)}, bf16[320,512]{1,0:T(8,128)(2,1)S(1)}, bf16[512,320]{1,0:T(8,128)(2,1)S(1)}, bf16...) custom-call(bf16[192,1296]{1,0:T(8,128)(2,1)S(1)} %get-tuple-element, ...), custom_call_target="tpu_custom_call" | custom-call | flops 238878720 | bytes 6000000 | tf_op jit(solution)/shard_map/tail/pallas_call | solution.py:358
  8.7 0.0 collective-permute-done.sxa
  8.7 0.7 collective-permute-done.1.sxb
  9.4 6.8 %collective-permute-start.3 = (f32[96,128]{1,0:T(8,128)S(1)}, f32[96,128]{1,0:T(8,128)S(1)}, u32[]{:S(2)}, u32[]{:S(2)}) collective-permute-start(f32[96,128]{1,0:T(8,128)S(1)} %get-tuple-element.104), channel_id=1, source_target_pairs={{1,2},{3,4},{5,6},{7,8},{9,10},{11,12},{13,14},{15,16},{17,18},{19... | collective-permute-start | bytes 147464 | tf_op jit(solution)/shard_map/ppermute | solution.py:320
  16.2 0.0 collective-permute-start.2
  16.2 0.9 %head.1 = f32[96,512]{1,0:T(8,128)S(1)} custom-call(bf16[192,1296]{1,0:T(8,128)(2,1)S(1)} %get-tuple-element.54.field, f32[256,256]{1,0:T(8,128)S(1)} %get-tuple-element.61.slab0, f32[256,512]{1,0:T(8,128)S(1)} %get-tuple-element.62.slab1), custom_call_target="tpu_custom_call" | custom-call | flops 226492416 | bytes 1200000 | tf_op jit(solution)/shard_map/head/pallas_call | solution.py:394
  17.1 2.0 %side.1 = (f32[96,128]{1,0:T(8,128)S(1)}, f32[96,128]{1,0:T(8,128)S(1)}, bf16[512,1296]{1,0:T(8,128)(2,1)S(1)}, bf16[512,512]{1,0:T(8,128)(2,1)S(1)}, bf16[256,1...) custom-call(s32[8,128]{1,0:T(8,128)S(1)} %add.71.odd, ...), custom_call_target="tpu_custom_call" | custom-call | flops 382205952 | bytes 3000000 | tf_op jit(solution)/shard_map/side/pallas_call | solution.py:374
  19.1 0.0 collective-permute-done.3.syb
  19.1 0.3 collective-permute-done.2.sya
  19.4 0.6 halo.1
  20.0 1.3 %collective-permute-start.4 = (f32[192,128]{1,0:T(8,128)S(1)}, f32[192,128]{1,0:T(8,128)S(1)}, u32[]{:S(2)}, u32[]{:S(2)}) collective-permute-start(f32[192,128]{1,0:T(8,128)S(1)} %get-tuple-element.75), channel_id=1, source_target_pairs={{0,1},{1,0},{2,3},{3,2},{4,5},{5,4},{6,7},{7,6},{8,9},{9,8},{10,11... | collective-permute-start | bytes 294920 | tf_op jit(solution)/shard_map/ppermute | solution.py:314
  21.3 1.9 %collective-permute-start.5 = (f32[96,128]{1,0:T(8,128)S(1)}, f32[96,128]{1,0:T(8,128)S(1)}, u32[]{:S(2)}, u32[]{:S(2)}) collective-permute-start(f32[96,128]{1,0:T(8,128)S(1)} %get-tuple-element.76), channel_id=1, source_target_pairs={{1,2},{3,4},{5,6},{7,8},{9,10},{11,12},{13,14},{15,16},{17,18},{19... | collective-permute-start | bytes 147464 | tf_op jit(solution)/shard_map/ppermute | solution.py:320
  23.3 3.0 %last.1.own_part = f32[96,1280]{1,0:T(8,128)S(1)} custom-call(bf16[192,1296]{1,0:T(8,128)(2,1)S(1)} %get-tuple-element.54.field, f32[256,768]{1,0:T(8,128)S(1)} %get-tuple-element.77.slab2, f32[256,1024]{1,0:T(8,128)S(1)} %get-tuple-element.78.slab3, f32[96,512]{1,0:T(8,128)S(1)} %head.1, f32[1,1,1600,1600]{3,2,1,0:T(8,128)} %factor.7), custom_call_target="tpu_custom_call" | custom-call | flops 905969664 | bytes 3000000 | tf_op jit(solution)/shard_map/last/pallas_call | solution.py:415
  26.3 1.3 %collective-permute-done.5.ryb = f32[96,128]{1,0:T(8,128)S(1)} collective-permute-done((f32[96,128]{1,0:T(8,128)S(1)}, f32[96,128]{1,0:T(8,128)S(1)}, u32[]{:S(2)}, u32[]{:S(2)}) %collective-permute-start.5) | collective-permute-done | bytes 49184 | tf_op jit(solution)/shard_map/ppermute | solution.py:320
  27.6 0.0 collective-permute-done.4.rya
  27.6 2.7 %collective-permute-start.7 = (f32[96,128]{1,0:T(8,128)S(1)}, f32[96,128]{1,0:T(8,128)S(1)}, u32[]{:S(2)}, u32[]{:S(2)}) collective-permute-start(f32[96,128]{1,0:T(8,128)S(1)} %get-tuple-element.102), channel_id=1, source_target_pairs={{32,64},{96,128},{160,192},{224,0},{64,32},{128,96},{192,160},{0,2... | collective-permute-start | bytes 147464 | tf_op jit(solution)/shard_map/ppermute | solution.py:320
  30.3 1.6 %collective-permute-start.6 = (f32[96,128]{1,0:T(8,128)S(1)}, f32[96,128]{1,0:T(8,128)S(1)}, u32[]{:S(2)}, u32[]{:S(2)}) collective-permute-start(f32[96,128]{1,0:T(8,128)S(1)} %get-tuple-element.103), channel_id=1, source_target_pairs={{0,32},{32,0},{64,96},{96,64},{128,160},{160,128},{192,224},{224,1... | collective-permute-start | bytes 147464 | tf_op jit(solution)/shard_map/ppermute | solution.py:314
  31.9 1.8 %local.1 = (f32[96,1296]{1,0:T(8,128)S(1)}, f32[96,512]{1,0:T(8,128)S(1)}, f32[288,96]{1,0:T(8,128)S(1)}) custom-call(f32[96,1280]{1,0:T(8,128)S(1)} %last.1.own_part, f32[96,320]{1,0:T(8,128)S(1)} %get-tuple-element.85.half, bf16[320,1296]{1,0:T(8,128)(2,1)S(1)} %get-tuple-element.86.oh, bf16[320,1296]{1,0:T(8,128)(2,1)S(1)} %get-tuple-element.87.olo, ...), custom_call_target="tpu_custom_call" | custom-call | flops 821145600 | bytes 4000000 | tf_op jit(solution)/shard_map/local/pallas_call | solution.py:429
  33.7 0.0 collective-permute-done.7.rxb
  33.7 0.0 collective-permute-done.6.rxa
  33.7 0.8 %gram.1 = (f32[144,128]{1,0:T(8,128)S(1)}, f32[144,128]{1,0:T(8,128)S(1)}, f32[96,512]{1,0:T(8,128)S(1)}) custom-call(s32[8,128]{1,0:T(8,128)S(1)} %add.71.odd, f32[96,128]{1,0:T(8,128)S(1)} %collective-permute-done.6.rxa, f32[96,128]{1,0:T(8,128)S(1)} %collective-permute-done.7.rxb, f32[192,128]{1,0:T(8,128)S(1)} %collective-permute-done.4.rya, ...), custom_call_target="tpu_custom_call" | custom-call | flops 265420800 | bytes 2000000 | tf_op jit(solution)/shard_map/gram/pallas_call | solution.py:438
  34.5 2.6 %collective-permute-start.8 = (f32[144,128]{1,0:T(8,128)S(1)}, f32[144,128]{1,0:T(8,128)S(1)}, u32[]{:S(2)}, u32[]{:S(2)}) collective-permute-start(f32[144,128]{1,0:T(8,128)S(1)} %get-tuple-element.97), channel_id=1, source_target_pairs={{0,32},{32,0},{64,96},{96,64},{128,160},{160,128},{192,224},{224,1... | collective-permute-start | bytes 221192 | tf_op jit(solution)/shard_map/ppermute | solution.py:314
  37.1 0.9 %collective-permute-done.8 = f32[144,128]{1,0:T(8,128)S(1)} collective-permute-done((f32[144,128]{1,0:T(8,128)S(1)}, f32[144,128]{1,0:T(8,128)S(1)}, u32[]{:S(2)}, u32[]{:S(2)}) %collective-permute-start.8) | collective-permute-done | bytes 73760 | tf_op jit(solution)/shard_map/ppermute | solution.py:314
  38.0 0.1 collective-permute-start.11
  38.1 0.2 collective-permute-start.10
  38.3 2.5 %collective-permute-start.9 = (f32[144,128]{1,0:T(8,128)S(1)}, f32[144,128]{1,0:T(8,128)S(1)}, u32[]{:S(2)}, u32[]{:S(2)}) collective-permute-start(f32[144,128]{1,0:T(8,128)S(1)} %add.78), channel_id=1, source_target_pairs={{0,64},{1,65},{2,66},{3,67},{4,68},{5,69},{6,70},{7,71},{8,72},{9,... | collective-permute-start | bytes 221192 | tf_op jit(solution)/shard_map/ppermute | solution.py:474
  40.8 2.2 %collective-permute-done.11 = f32[144,128]{1,0:T(8,128)S(1)} collective-permute-done((f32[144,128]{1,0:T(8,128)S(1)}, f32[144,128]{1,0:T(8,128)S(1)}, u32[]{:S(2)}, u32[]{:S(2)}) %collective-permute-start.11) | collective-permute-done | bytes 73760 | tf_op jit(solution)/shard_map/ppermute | solution.py:474
  42.9 0.8 %collective-permute-done.10 = f32[144,128]{1,0:T(8,128)S(1)} collective-permute-done((f32[144,128]{1,0:T(8,128)S(1)}, f32[144,128]{1,0:T(8,128)S(1)}, u32[]{:S(2)}, u32[]{:S(2)}) %collective-permute-start.10) | collective-permute-done | bytes 73760 | tf_op jit(solution)/shard_map/ppermute | solution.py:474
  43.7 0.0 collective-permute-done.9
  43.7 0.1 collective-permute-start.14
  43.8 0.4 collective-permute-start.13
  44.3 2.2 %collective-permute-start.12 = (f32[144,128]{1,0:T(8,128)S(1)}, f32[144,128]{1,0:T(8,128)S(1)}, u32[]{:S(2)}, u32[]{:S(2)}) collective-permute-start(f32[144,128]{1,0:T(8,128)S(1)} %add_add_fusion.1), channel_id=1, source_target_pairs={{0,8},{1,9},{2,10},{3,11},{4,12},{5,13},{6,14},{7,15},{8,0},{9,1},... | collective-permute-start | bytes 221192 | tf_op jit(solution)/shard_map/ppermute | solution.py:474
  46.5 2.2 %collective-permute-done.14 = f32[144,128]{1,0:T(8,128)S(1)} collective-permute-done((f32[144,128]{1,0:T(8,128)S(1)}, f32[144,128]{1,0:T(8,128)S(1)}, u32[]{:S(2)}, u32[]{:S(2)}) %collective-permute-start.14) | collective-permute-done | bytes 73760 | tf_op jit(solution)/shard_map/ppermute | solution.py:474
  48.6 0.5 collective-permute-done.13
  49.1 0.0 collective-permute-done.12
  49.2 0.1 collective-permute-start.15
  49.3 1.3 %update.1 = f32[96,1296]{1,0:T(8,128)} custom-call(f32[96,512]{1,0:T(8,128)S(1)} %get-tuple-element.98.back, bf16[512,1296]{1,0:T(8,128)(2,1)S(1)} %get-tuple-element.88.turned, f32[96,1296]{1,0:T(8,128)S(1)} %get-tuple-element.99.local), custom_call_target="tpu_custom_call" | custom-call | flops 254803968 | bytes 3000000 | tf_op jit(solution)/shard_map/update/pallas_call | solution.py:447
  50.6 4.1 %collective-permute-done.15 = f32[144,128]{1,0:T(8,128)S(1)} collective-permute-done((f32[144,128]{1,0:T(8,128)S(1)}, f32[144,128]{1,0:T(8,128)S(1)}, u32[]{:S(2)}, u32[]{:S(2)}) %collective-permute-start.15) | collective-permute-done | bytes 73760 | tf_op jit(solution)/shard_map/ppermute | solution.py:314
  54.7 0.1 collective-permute-start.17
  54.8 0.1 collective-permute-start.18
  54.9 2.5 %collective-permute-start.16 = (f32[144,128]{1,0:T(8,128)S(1)}, f32[144,128]{1,0:T(8,128)S(1)}, u32[]{:S(2)}, u32[]{:S(2)}) collective-permute-start(f32[144,128]{1,0:T(8,128)S(1)} %add.85), channel_id=1, source_target_pairs={{0,1},{1,0},{2,3},{3,2},{4,5},{5,4},{6,7},{7,6},{8,9},{9,8},{10,11... | collective-permute-start | bytes 221192 | tf_op jit(solution)/shard_map/ppermute | solution.py:314
  57.4 1.5 %collective-permute-done.17 = f32[144,128]{1,0:T(8,128)S(1)} collective-permute-done((f32[144,128]{1,0:T(8,128)S(1)}, f32[144,128]{1,0:T(8,128)S(1)}, u32[]{:S(2)}, u32[]{:S(2)}) %collective-permute-start.17) | collective-permute-done | bytes 73760 | tf_op jit(solution)/shard_map/ppermute | solution.py:314
  58.9 1.1 %collective-permute-done.18 = f32[144,128]{1,0:T(8,128)S(1)} collective-permute-done((f32[144,128]{1,0:T(8,128)S(1)}, f32[144,128]{1,0:T(8,128)S(1)}, u32[]{:S(2)}, u32[]{:S(2)}) %collective-permute-start.18) | collective-permute-done | bytes 73760 | tf_op jit(solution)/shard_map/ppermute | solution.py:314
  60.0 0.4 collective-permute-done.16
  60.5 4.6 %collective-permute-start.19 = (f32[192,128]{1,0:T(8,128)S(1)}, f32[192,128]{1,0:T(8,128)S(1)}, u32[]{:S(2)}, u32[]{:S(2)}) collective-permute-start(f32[192,128]{1,0:T(8,128)S(1)} %pad_maximum_fusion.refs_0_), channel_id=1, source_target_pairs={{0,32},{32,0},{64,96},{96,64},{128,160},{160,128},{192,224},{224,1... | collective-permute-start | bytes 294920 | tf_op jit(solution)/shard_map/ppermute | solution.py:314
  65.1 0.9 %collective-permute-done.19.refs_1_ = f32[192,128]{1,0:T(8,128)S(1)} collective-permute-done((f32[192,128]{1,0:T(8,128)S(1)}, f32[192,128]{1,0:T(8,128)S(1)}, u32[]{:S(2)}, u32[]{:S(2)}) %collective-permute-start.19) | collective-permute-done | bytes 98336 | tf_op jit(solution)/shard_map/ppermute | solution.py:314
  66.1 1.1 %final.1 = f32[288,288]{1,0:T(8,128)} custom-call(s32[8,128]{1,0:T(8,128)S(1)} %add.71.odd, f32[192,128]{1,0:T(8,128)S(1)} %pad_maximum_fusion.refs_0_, f32[192,128]{1,0:T(8,128)S(1)} %collective-permute-done.19.refs_1_), custom_call_target="tpu_custom_call" | custom-call | flops 1000000 | bytes 700000 | tf_op jit(solution)/shard_map/final/pallas_call | solution.py:496
  (12 shorter events, 0.1 us)
Async XLA Ops:
  2.6 6.2 %collective-permute-start = (f32[96,128]{1,0:T(8,128)S(1)}, f32[96,128]{1,0:T(8,128)S(1)}, u32[]{:S(2)}, u32[]{:S(2)}) collective-permute-start(f32[96,128]{1,0:T(8,128)S(1)} %get-tuple-element.52), channel_id=1, source_target_pairs={{0,32},{32,0},{64,96},{96,64},{128,160},{160,128},{192,224},{224,1... | collective-permute-start | bytes 147464 | tf_op jit(solution)/shard_map/ppermute | solution.py:314
  5.9 3.5 %collective-permute-start.1 = (f32[96,128]{1,0:T(8,128)S(1)}, f32[96,128]{1,0:T(8,128)S(1)}, u32[]{:S(2)}, u32[]{:S(2)}) collective-permute-start(f32[96,128]{1,0:T(8,128)S(1)} %get-tuple-element.53), channel_id=1, source_target_pairs={{32,64},{96,128},{160,192},{224,0},{64,32},{128,96},{192,160},{0,2... | collective-permute-start | bytes 147464 | tf_op jit(solution)/shard_map/ppermute | solution.py:320
  9.4 9.7 %collective-permute-start.3 = (f32[96,128]{1,0:T(8,128)S(1)}, f32[96,128]{1,0:T(8,128)S(1)}, u32[]{:S(2)}, u32[]{:S(2)}) collective-permute-start(f32[96,128]{1,0:T(8,128)S(1)} %get-tuple-element.104), channel_id=1, source_target_pairs={{1,2},{3,4},{5,6},{7,8},{9,10},{11,12},{13,14},{15,16},{17,18},{19... | collective-permute-start | bytes 147464 | tf_op jit(solution)/shard_map/ppermute | solution.py:320
  16.2 3.2 %collective-permute-start.2 = (f32[96,128]{1,0:T(8,128)S(1)}, f32[96,128]{1,0:T(8,128)S(1)}, u32[]{:S(2)}, u32[]{:S(2)}) collective-permute-start(f32[96,128]{1,0:T(8,128)S(1)} %get-tuple-element.105), channel_id=1, source_target_pairs={{0,1},{1,0},{2,3},{3,2},{4,5},{5,4},{6,7},{7,6},{8,9},{9,8},{10,11... | collective-permute-start | bytes 147464 | tf_op jit(solution)/shard_map/ppermute | solution.py:314
  20.0 7.5 %collective-permute-start.4 = (f32[192,128]{1,0:T(8,128)S(1)}, f32[192,128]{1,0:T(8,128)S(1)}, u32[]{:S(2)}, u32[]{:S(2)}) collective-permute-start(f32[192,128]{1,0:T(8,128)S(1)} %get-tuple-element.75), channel_id=1, source_target_pairs={{0,1},{1,0},{2,3},{3,2},{4,5},{5,4},{6,7},{7,6},{8,9},{9,8},{10,11... | collective-permute-start | bytes 294920 | tf_op jit(solution)/shard_map/ppermute | solution.py:314
  21.3 6.3 %collective-permute-start.5 = (f32[96,128]{1,0:T(8,128)S(1)}, f32[96,128]{1,0:T(8,128)S(1)}, u32[]{:S(2)}, u32[]{:S(2)}) collective-permute-start(f32[96,128]{1,0:T(8,128)S(1)} %get-tuple-element.76), channel_id=1, source_target_pairs={{1,2},{3,4},{5,6},{7,8},{9,10},{11,12},{13,14},{15,16},{17,18},{19... | collective-permute-start | bytes 147464 | tf_op jit(solution)/shard_map/ppermute | solution.py:320
  27.6 6.1 %collective-permute-start.7 = (f32[96,128]{1,0:T(8,128)S(1)}, f32[96,128]{1,0:T(8,128)S(1)}, u32[]{:S(2)}, u32[]{:S(2)}) collective-permute-start(f32[96,128]{1,0:T(8,128)S(1)} %get-tuple-element.102), channel_id=1, source_target_pairs={{32,64},{96,128},{160,192},{224,0},{64,32},{128,96},{192,160},{0,2... | collective-permute-start | bytes 147464 | tf_op jit(solution)/shard_map/ppermute | solution.py:320
  30.3 3.4 %collective-permute-start.6 = (f32[96,128]{1,0:T(8,128)S(1)}, f32[96,128]{1,0:T(8,128)S(1)}, u32[]{:S(2)}, u32[]{:S(2)}) collective-permute-start(f32[96,128]{1,0:T(8,128)S(1)} %get-tuple-element.103), channel_id=1, source_target_pairs={{0,32},{32,0},{64,96},{96,64},{128,160},{160,128},{192,224},{224,1... | collective-permute-start | bytes 147464 | tf_op jit(solution)/shard_map/ppermute | solution.py:314
  34.5 3.5 %collective-permute-start.8 = (f32[144,128]{1,0:T(8,128)S(1)}, f32[144,128]{1,0:T(8,128)S(1)}, u32[]{:S(2)}, u32[]{:S(2)}) collective-permute-start(f32[144,128]{1,0:T(8,128)S(1)} %get-tuple-element.97), channel_id=1, source_target_pairs={{0,32},{32,0},{64,96},{96,64},{128,160},{160,128},{192,224},{224,1... | collective-permute-start | bytes 221192 | tf_op jit(solution)/shard_map/ppermute | solution.py:314
  38.0 4.9 %collective-permute-start.11 = (f32[144,128]{1,0:T(8,128)S(1)}, f32[144,128]{1,0:T(8,128)S(1)}, u32[]{:S(2)}, u32[]{:S(2)}) collective-permute-start(f32[144,128]{1,0:T(8,128)S(1)} %add.78), channel_id=1, source_target_pairs={{0,128},{1,129},{2,130},{3,131},{4,132},{5,133},{6,134},{7,135},{8... | collective-permute-start | bytes 221192 | tf_op jit(solution)/shard_map/ppermute | solution.py:474
  38.1 5.6 %collective-permute-start.10 = (f32[144,128]{1,0:T(8,128)S(1)}, f32[144,128]{1,0:T(8,128)S(1)}, u32[]{:S(2)}, u32[]{:S(2)}) collective-permute-start(f32[144,128]{1,0:T(8,128)S(1)} %add.78), channel_id=1, source_target_pairs={{0,192},{1,193},{2,194},{3,195},{4,196},{5,197},{6,198},{7,199},{8... | collective-permute-start | bytes 221192 | tf_op jit(solution)/shard_map/ppermute | solution.py:474
  38.3 5.4 %collective-permute-start.9 = (f32[144,128]{1,0:T(8,128)S(1)}, f32[144,128]{1,0:T(8,128)S(1)}, u32[]{:S(2)}, u32[]{:S(2)}) collective-permute-start(f32[144,128]{1,0:T(8,128)S(1)} %add.78), channel_id=1, source_target_pairs={{0,64},{1,65},{2,66},{3,67},{4,68},{5,69},{6,70},{7,71},{8,72},{9,... | collective-permute-start | bytes 221192 | tf_op jit(solution)/shard_map/ppermute | solution.py:474
  43.7 4.9 %collective-permute-start.14 = (f32[144,128]{1,0:T(8,128)S(1)}, f32[144,128]{1,0:T(8,128)S(1)}, u32[]{:S(2)}, u32[]{:S(2)}) collective-permute-start(f32[144,128]{1,0:T(8,128)S(1)} %add_add_fusion.1), channel_id=1, source_target_pairs={{0,16},{1,17},{2,18},{3,19},{4,20},{5,21},{6,22},{7,23},{8,24},{9,... | collective-permute-start | bytes 221192 | tf_op jit(solution)/shard_map/ppermute | solution.py:474
  43.8 5.3 %collective-permute-start.13 = (f32[144,128]{1,0:T(8,128)S(1)}, f32[144,128]{1,0:T(8,128)S(1)}, u32[]{:S(2)}, u32[]{:S(2)}) collective-permute-start(f32[144,128]{1,0:T(8,128)S(1)} %add_add_fusion.1), channel_id=1, source_target_pairs={{0,24},{1,25},{2,26},{3,27},{4,28},{5,29},{6,30},{7,31},{8,16},{9,... | collective-permute-start | bytes 221192 | tf_op jit(solution)/shard_map/ppermute | solution.py:474
  44.3 4.9 %collective-permute-start.12 = (f32[144,128]{1,0:T(8,128)S(1)}, f32[144,128]{1,0:T(8,128)S(1)}, u32[]{:S(2)}, u32[]{:S(2)}) collective-permute-start(f32[144,128]{1,0:T(8,128)S(1)} %add_add_fusion.1), channel_id=1, source_target_pairs={{0,8},{1,9},{2,10},{3,11},{4,12},{5,13},{6,14},{7,15},{8,0},{9,1},... | collective-permute-start | bytes 221192 | tf_op jit(solution)/shard_map/ppermute | solution.py:474
  49.2 5.5 %collective-permute-start.15 = (f32[144,128]{1,0:T(8,128)S(1)}, f32[144,128]{1,0:T(8,128)S(1)}, u32[]{:S(2)}, u32[]{:S(2)}) collective-permute-start(f32[144,128]{1,0:T(8,128)S(1)} %add_add_fusion), channel_id=1, source_target_pairs={{0,6},{1,7},{2,4},{3,5},{4,2},{5,3},{6,0},{7,1},{8,14},{9,15},{10,... | collective-permute-start | bytes 221192 | tf_op jit(solution)/shard_map/ppermute | solution.py:314
  54.7 4.2 %collective-permute-start.17 = (f32[144,128]{1,0:T(8,128)S(1)}, f32[144,128]{1,0:T(8,128)S(1)}, u32[]{:S(2)}, u32[]{:S(2)}) collective-permute-start(f32[144,128]{1,0:T(8,128)S(1)} %add.85), channel_id=1, source_target_pairs={{0,2},{1,3},{2,0},{3,1},{4,6},{5,7},{6,4},{7,5},{8,10},{9,11},{10,... | collective-permute-start | bytes 221192 | tf_op jit(solution)/shard_map/ppermute | solution.py:314
  54.8 5.3 %collective-permute-start.18 = (f32[144,128]{1,0:T(8,128)S(1)}, f32[144,128]{1,0:T(8,128)S(1)}, u32[]{:S(2)}, u32[]{:S(2)}) collective-permute-start(f32[144,128]{1,0:T(8,128)S(1)} %add.85), channel_id=1, source_target_pairs={{0,3},{1,2},{2,1},{3,0},{4,7},{5,6},{6,5},{7,4},{8,11},{9,10},{10,... | collective-permute-start | bytes 221192 | tf_op jit(solution)/shard_map/ppermute | solution.py:314
  54.9 5.6 %collective-permute-start.16 = (f32[144,128]{1,0:T(8,128)S(1)}, f32[144,128]{1,0:T(8,128)S(1)}, u32[]{:S(2)}, u32[]{:S(2)}) collective-permute-start(f32[144,128]{1,0:T(8,128)S(1)} %add.85), channel_id=1, source_target_pairs={{0,1},{1,0},{2,3},{3,2},{4,5},{5,4},{6,7},{7,6},{8,9},{9,8},{10,11... | collective-permute-start | bytes 221192 | tf_op jit(solution)/shard_map/ppermute | solution.py:314
  60.5 5.6 %collective-permute-start.19 = (f32[192,128]{1,0:T(8,128)S(1)}, f32[192,128]{1,0:T(8,128)S(1)}, u32[]{:S(2)}, u32[]{:S(2)}) collective-permute-start(f32[192,128]{1,0:T(8,128)S(1)} %pad_maximum_fusion.refs_0_), channel_id=1, source_target_pairs={{0,32},{32,0},{64,96},{96,64},{128,160},{160,128},{192,224},{224,1... | collective-permute-start | bytes 294920 | tf_op jit(solution)/shard_map/ppermute | solution.py:314
where the time goes:
time: 68 us; the launch traced here: 67.4 us
  starting transfers between devices  33.2 us (49%)
  waiting for transfers between devices  16.8 us (25%)
  Pallas kernels  16.2 us (24%)
  between operations  0.99 us (1%)
    ppermute x10, starting transfers between devices, swap(): lax.ppermute(block, axis, [(i, i ^ step) for i in range(lax.axis_size(axi...  16.3 us
    ppermute x4, starting transfers between devices, swap_odd(): return lax.ppermute(block, axis, route + [(b, a) for a, b in route])  11.4 us
    ppermute x10, waiting for transfers between devices, swap(): lax.ppermute(block, axis, [(i, i ^ step) for i in range(lax.axis_size(axi...  9.28 us
    ppermute x6, waiting for transfers between devices, moved(): return lax.ppermute(value, ('sx', 'sy'), route)  5.61 us
    ppermute x6, starting transfers between devices, moved(): return lax.ppermute(value, ('sx', 'sy'), route)  5.46 us
    pallas_call x1, Pallas kernels, body(): call(last_kernel, shaped(96, TAIL), [VMEM] * 4 + [HBM], [pltpu.VMEM((256,...  3.03 us
    pallas_call x1, Pallas kernels, body(): call(tail_kernel, (shaped(96, 320), placed, placed, turned, turned, wide,...  2.83 us
    pallas_call x1, Pallas kernels, body(): call(side_kernel, (msg, msg, shaped(512, own, dtype=BF16), shaped(512, 51...  1.98 us
  transfers between devices with their start and end apart: 20, of which 13 were waited for; matrix products, arithmetic and copies ran while one was open for 0% of the time, Pallas kernels for 18%

commit v1 on v0

--- a/solution.py
+++ b/solution.py
@@ -64,7 +64,7 @@
 
 
 def gather_kernel(
-    odd, count_hbm, rows_hbm, res_hbm, factor, sxa, sxb, sya, syb, field, ids, slab, count, rows, res, sem
+    odd, count_hbm, rows_hbm, res_hbm, factor, sxb, sxa, sya, syb, field, ids, slab, count, rows, res, sem
 ):
     fetch_count = pltpu.make_async_copy(count_hbm, count, sem.at[0])
     fetch_rows = pltpu.make_async_copy(rows_hbm, rows, sem.at[1])
@@ -328,7 +328,7 @@
     msg = shaped(96, LANES)
 
     factor = in_hbm(inverse_factor)
-    sxa, sxb, sya, syb, field, ids, slab = call(
+    sxb, sxa, sya, syb, field, ids, slab = call(
         gather_kernel,
         (
             msg,
@@ -365,9 +365,9 @@
         moved=6000000,
         name="tail",
     )(field, slab, factor, in_hbm(ritz_block), in_hbm(search_block))
-    gxa, gxb, part = lax.optimization_barrier((gxa, gxb, part))
-
-    relay = jnp.where(lane >= EDGE, gxa + gxb, 0.0)
+    gxb, gxa, part = lax.optimization_barrier((gxb, gxa, part))
+
+    relay = jnp.where(lane >= EDGE, gxb + gxa, 0.0)
     gyb, gya = swap_odd(syb + relay, "sy"), swap(sya + relay, "sy", 1)
 
     sides, sent_sides = shaped(2 * LANES, own, dtype=BF16), shaped(512, 2 * LANES, dtype=BF16)
@@ -453,37 +453,32 @@
         name="update",
     )(back, turned, local)
 
-    def summed(value, axis, steps):
-        total = swap(value, axis, steps[0])
-        for step in steps[1:]:
-            total = total + swap(value, axis, step)
+    rows, cols = lax.axis_size("sx"), lax.axis_size("sy")
+
+    def swap_apart(value, even_core, odd_core):
+        route = []
+        for r in range(rows):
+            for c in range(cols):
+                row_step, col_step = odd_core if r % 2 else even_core
+                route.append((r * cols + c, (r ^ row_step) * cols + (c ^ col_step)))
+        return lax.ppermute(value, ("sx", "sy"), route)
+
+    def summed(value, even_cores, odd_cores):
+        total = swap_apart(value, even_cores[0], odd_cores[0])
+        for even_core, odd_core in zip(even_cores[1:], odd_cores[1:]):
+            total = total + swap_apart(value, even_core, odd_core)
         return value + total
 
-    def summed_apart(value, first):
-        rows, cols = lax.axis_size("sx"), lax.axis_size("sy")
-
-        def partner(r, c, step):
-            return (r ^ (2 * step), c) if r % 2 == first else (r, c ^ (8 * step))
-
-        def moved(step):
-            route = []
-            for r in range(rows):
-                for c in range(cols):
-                    to_row, to_col = partner(r, c, step)
-                    route.append((r * cols + c, to_row * cols + to_col))
-            return lax.ppermute(value, ("sx", "sy"), route)
-
-        total = moved(1)
-        for step in (3, 2):
-            total = total + moved(step)
-        return value + total
-
+    along_y = [(2 * step, 0) for step in (1, 3, 2)]
+    along_x = [(0, 8 * step) for step in (1, 3, 2)]
     total = kept + swap(away, "sx", 1)
-    total = summed_apart(total, 0)
-    total = summed_apart(total, 1)
-    total = summed(total, "sy", (6,))
+    total = summed(total, along_y, along_x)
+    total = summed(total, along_x, along_y)
+    total = summed(total, [(0, 6)], [(0, 2)])
     total, precond = lax.optimization_barrier((total, precond))
-    three, two, one = (swap(total, "sy", step) for step in (3, 2, 1))
+    three = swap_apart(total, (0, 3), (0, 7))
+    two = swap_apart(total, (0, 2), (0, 6))
+    one = swap_apart(total, (0, 1), (0, 1))
     late = (total[:96] + one[:96]) + (two[:96] + three[:96])
     mine = jnp.concatenate([late, total[96:] + two[96:], one[96:] + three[96:]], axis=0)
     other = swap(mine, "sx", 1)

time: 68 us -> 67.1 us (0.987)
  waiting for transfers between devices: 16.8 us -> 13.9 us
  starting transfers between devices: 33.2 us -> 35.6 us
    ppermute x10 -> x6, waiting for transfers between devices: 9.28 us -> 1.87 us  [swap(): lax.ppermute(block, axis, [(i, i ^ step) for i in range(lax.axis_size(axi...]
    ppermute x10 -> x6, starting transfers between devices: 16.3 us -> 9.75 us  [swap(): lax.ppermute(block, axis, [(i, i ^ step) for i in range(lax.axis_size(axi...]
    ppermute x6 -> x10, waiting for transfers between devices: 5.61 us -> 11.2 us  [swap_apart(): return lax.ppermute(value, ('sx', 'sy'), route)]
    ppermute x6 -> x10, starting transfers between devices: 5.46 us -> 10.4 us  [swap_apart(): return lax.ppermute(value, ('sx', 'sy'), route)]
    ppermute x4, starting transfers between devices: 11.4 us -> 15.5 us  [swap_odd(): return lax.ppermute(block, axis, route + [(b, a) for a, b in route])]
    ppermute x4, waiting for transfers between devices: 1.95 us -> 0.87 us  [swap_odd(): return lax.ppermute(block, axis, route + [(b, a) for a, b in route])]
  transfers between devices with their start and end apart: 20 -> 20, of which waited for: 13 -> 11; matrix products, arithmetic and copies ran while one was open for 0% -> 0% of each run, Pallas kernels for 18% -> 18%
where the time goes in v1:
time: 67.1 us; the launch traced here: 66.9 us
  starting transfers between devices  35.6 us (53%)
  Pallas kernels  16.2 us (24%)
  waiting for transfers between devices  13.9 us (21%)
  between operations  1 us (1%)
    ppermute x4, starting transfers between devices, swap_odd(): return lax.ppermute(block, axis, route + [(b, a) for a, b in route])  15.5 us
    ppermute x10, waiting for transfers between devices, swap_apart(): return lax.ppermute(value, ('sx', 'sy'), route)  11.2 us
    ppermute x10, starting transfers between devices, swap_apart(): return lax.ppermute(value, ('sx', 'sy'), route)  10.4 us
    ppermute x6, starting transfers between devices, swap(): lax.ppermute(block, axis, [(i, i ^ step) for i in range(lax.axis_size(axi...  9.75 us
    pallas_call x1, Pallas kernels, body(): call(last_kernel, shaped(96, TAIL), [VMEM] * 4 + [HBM], [pltpu.VMEM((256,...  3.03 us
    pallas_call x1, Pallas kernels, body(): call(tail_kernel, (shaped(96, 320), placed, placed, turned, turned, wide,...  2.83 us
    pallas_call x1, Pallas kernels, body(): call(side_kernel, (msg, msg, shaped(512, own, dtype=BF16), shaped(512, 51...  1.98 us
    ppermute x6, waiting for transfers between devices, swap(): lax.ppermute(block, axis, [(i, i ^ step) for i in range(lax.axis_size(axi...  1.87 us
  transfers between devices with their start and end apart: 20, of which 11 were waited for; matrix products, arithmetic and copies ran while one was open for 0% of the time, Pallas kernels for 18%

profile of v1, /device:TPU:1, one launch (start us, length us, event | category | flops | bytes accessed | tf_op | source)
XLA Modules:
  0.0 66.9 jit_solution(16602897260038213656)
XLA Ops:
  0.7 0.1 add.71.odd
  0.7 1.8 %gather.1 = (f32[96,128]{1,0:T(8,128)S(1)}, f32[96,128]{1,0:T(8,128)S(1)}, f32[96,128]{1,0:T(8,128)S(1)}, f32[96,128]{1,0:T(8,128)S(1)}, bf16[192,1296]{1,0:T(8,...) custom-call(s32[8,128]{1,0:T(8,128)S(1)} %add.71.odd, s32[1,1,8]{2,1,0:T(1,128)} %count_hbm.1, ...), custom_call_target="tpu_custom_call" | custom-call | flops 254803968 | bytes 2000000 | tf_op jit(solution)/shard_map/gather/pallas_call | solution.py:331
  2.6 2.8 %collective-permute-start = (f32[96,128]{1,0:T(8,128)S(1)}, f32[96,128]{1,0:T(8,128)S(1)}, u32[]{:S(2)}, u32[]{:S(2)}) collective-permute-start(f32[96,128]{1,0:T(8,128)S(1)} %get-tuple-element.52), channel_id=1, source_target_pairs={{32,64},{96,128},{160,192},{224,0},{64,32},{128,96},{192,160},{0,2... | collective-permute-start | bytes 147464 | tf_op jit(solution)/shard_map/ppermute | solution.py:320
  5.3 1.3 %collective-permute-start.1 = (f32[96,128]{1,0:T(8,128)S(1)}, f32[96,128]{1,0:T(8,128)S(1)}, u32[]{:S(2)}, u32[]{:S(2)}) collective-permute-start(f32[96,128]{1,0:T(8,128)S(1)} %get-tuple-element.53), channel_id=1, source_target_pairs={{0,32},{32,0},{64,96},{96,64},{128,160},{160,128},{192,224},{224,1... | collective-permute-start | bytes 147464 | tf_op jit(solution)/shard_map/ppermute | solution.py:314
  6.6 2.8 %tail.1 = (f32[96,320]{1,0:T(8,128)S(1)}, bf16[320,512]{1,0:T(8,128)(2,1)S(1)}, bf16[320,512]{1,0:T(8,128)(2,1)S(1)}, bf16[512,320]{1,0:T(8,128)(2,1)S(1)}, bf16...) custom-call(bf16[192,1296]{1,0:T(8,128)(2,1)S(1)} %get-tuple-element, ...), custom_call_target="tpu_custom_call" | custom-call | flops 238878720 | bytes 6000000 | tf_op jit(solution)/shard_map/tail/pallas_call | solution.py:358
  9.5 0.0 collective-permute-done.sxb
  9.5 0.0 collective-permute-done.1.sxa
  9.5 7.9 %collective-permute-start.3 = (f32[96,128]{1,0:T(8,128)S(1)}, f32[96,128]{1,0:T(8,128)S(1)}, u32[]{:S(2)}, u32[]{:S(2)}) collective-permute-start(f32[96,128]{1,0:T(8,128)S(1)} %get-tuple-element.104), channel_id=1, source_target_pairs={{1,2},{3,4},{5,6},{7,8},{9,10},{11,12},{13,14},{15,16},{17,18},{19... | collective-permute-start | bytes 147464 | tf_op jit(solution)/shard_map/ppermute | solution.py:320
  17.4 0.0 collective-permute-start.2
  17.4 0.9 %head.1 = f32[96,512]{1,0:T(8,128)S(1)} custom-call(bf16[192,1296]{1,0:T(8,128)(2,1)S(1)} %get-tuple-element.54.field, f32[256,256]{1,0:T(8,128)S(1)} %get-tuple-element.61.slab0, f32[256,512]{1,0:T(8,128)S(1)} %get-tuple-element.62.slab1), custom_call_target="tpu_custom_call" | custom-call | flops 226492416 | bytes 1200000 | tf_op jit(solution)/shard_map/head/pallas_call | solution.py:394
  18.3 2.0 %side.1 = (f32[96,128]{1,0:T(8,128)S(1)}, f32[96,128]{1,0:T(8,128)S(1)}, bf16[512,1296]{1,0:T(8,128)(2,1)S(1)}, bf16[512,512]{1,0:T(8,128)(2,1)S(1)}, bf16[256,1...) custom-call(s32[8,128]{1,0:T(8,128)S(1)} %add.71.odd, ...), custom_call_target="tpu_custom_call" | custom-call | flops 382205952 | bytes 3000000 | tf_op jit(solution)/shard_map/side/pallas_call | solution.py:374
  20.3 0.0 collective-permute-done.3.syb
  20.3 0.0 collective-permute-done.2.sya
  20.3 0.6 halo.1
  20.9 1.6 %collective-permute-start.4 = (f32[192,128]{1,0:T(8,128)S(1)}, f32[192,128]{1,0:T(8,128)S(1)}, u32[]{:S(2)}, u32[]{:S(2)}) collective-permute-start(f32[192,128]{1,0:T(8,128)S(1)} %get-tuple-element.75), channel_id=1, source_target_pairs={{0,1},{1,0},{2,3},{3,2},{4,5},{5,4},{6,7},{7,6},{8,9},{9,8},{10,11... | collective-permute-start | bytes 294920 | tf_op jit(solution)/shard_map/ppermute | solution.py:314
  22.5 2.4 %collective-permute-start.5 = (f32[96,128]{1,0:T(8,128)S(1)}, f32[96,128]{1,0:T(8,128)S(1)}, u32[]{:S(2)}, u32[]{:S(2)}) collective-permute-start(f32[96,128]{1,0:T(8,128)S(1)} %get-tuple-element.76), channel_id=1, source_target_pairs={{1,2},{3,4},{5,6},{7,8},{9,10},{11,12},{13,14},{15,16},{17,18},{19... | collective-permute-start | bytes 147464 | tf_op jit(solution)/shard_map/ppermute | solution.py:320
  24.8 3.0 %last.1.own_part = f32[96,1280]{1,0:T(8,128)S(1)} custom-call(bf16[192,1296]{1,0:T(8,128)(2,1)S(1)} %get-tuple-element.54.field, f32[256,768]{1,0:T(8,128)S(1)} %get-tuple-element.77.slab2, f32[256,1024]{1,0:T(8,128)S(1)} %get-tuple-element.78.slab3, f32[96,512]{1,0:T(8,128)S(1)} %head.1, f32[1,1,1600,1600]{3,2,1,0:T(8,128)} %factor.7), custom_call_target="tpu_custom_call" | custom-call | flops 905969664 | bytes 3000000 | tf_op jit(solution)/shard_map/last/pallas_call | solution.py:415
  27.9 0.9 %collective-permute-done.5.ryb = f32[96,128]{1,0:T(8,128)S(1)} collective-permute-done((f32[96,128]{1,0:T(8,128)S(1)}, f32[96,128]{1,0:T(8,128)S(1)}, u32[]{:S(2)}, u32[]{:S(2)}) %collective-permute-start.5) | collective-permute-done | bytes 49184 | tf_op jit(solution)/shard_map/ppermute | solution.py:320
  28.7 0.0 collective-permute-done.4.rya
  28.8 2.5 %collective-permute-start.7 = (f32[96,128]{1,0:T(8,128)S(1)}, f32[96,128]{1,0:T(8,128)S(1)}, u32[]{:S(2)}, u32[]{:S(2)}) collective-permute-start(f32[96,128]{1,0:T(8,128)S(1)} %get-tuple-element.102), channel_id=1, source_target_pairs={{32,64},{96,128},{160,192},{224,0},{64,32},{128,96},{192,160},{0,2... | collective-permute-start | bytes 147464 | tf_op jit(solution)/shard_map/ppermute | solution.py:320
  31.3 0.0 collective-permute-start.6
  31.3 1.8 %local.1 = (f32[96,1296]{1,0:T(8,128)S(1)}, f32[96,512]{1,0:T(8,128)S(1)}, f32[288,96]{1,0:T(8,128)S(1)}) custom-call(f32[96,1280]{1,0:T(8,128)S(1)} %last.1.own_part, f32[96,320]{1,0:T(8,128)S(1)} %get-tuple-element.85.half, bf16[320,1296]{1,0:T(8,128)(2,1)S(1)} %get-tuple-element.86.oh, bf16[320,1296]{1,0:T(8,128)(2,1)S(1)} %get-tuple-element.87.olo, ...), custom_call_target="tpu_custom_call" | custom-call | flops 821145600 | bytes 4000000 | tf_op jit(solution)/shard_map/local/pallas_call | solution.py:429
  33.0 0.0 collective-permute-done.7.rxb
  33.1 0.0 collective-permute-done.6.rxa
  33.1 0.8 %gram.1 = (f32[144,128]{1,0:T(8,128)S(1)}, f32[144,128]{1,0:T(8,128)S(1)}, f32[96,512]{1,0:T(8,128)S(1)}) custom-call(s32[8,128]{1,0:T(8,128)S(1)} %add.71.odd, f32[96,128]{1,0:T(8,128)S(1)} %collective-permute-done.6.rxa, f32[96,128]{1,0:T(8,128)S(1)} %collective-permute-done.7.rxb, f32[192,128]{1,0:T(8,128)S(1)} %collective-permute-done.4.rya, ...), custom_call_target="tpu_custom_call" | custom-call | flops 265420800 | bytes 2000000 | tf_op jit(solution)/shard_map/gram/pallas_call | solution.py:438
  33.8 2.6 %collective-permute-start.8 = (f32[144,128]{1,0:T(8,128)S(1)}, f32[144,128]{1,0:T(8,128)S(1)}, u32[]{:S(2)}, u32[]{:S(2)}) collective-permute-start(f32[144,128]{1,0:T(8,128)S(1)} %get-tuple-element.97), channel_id=1, source_target_pairs={{0,32},{32,0},{64,96},{96,64},{128,160},{160,128},{192,224},{224,1... | collective-permute-start | bytes 221192 | tf_op jit(solution)/shard_map/ppermute | solution.py:314
  36.4 0.9 %collective-permute-done.8 = f32[144,128]{1,0:T(8,128)S(1)} collective-permute-done((f32[144,128]{1,0:T(8,128)S(1)}, f32[144,128]{1,0:T(8,128)S(1)}, u32[]{:S(2)}, u32[]{:S(2)}) %collective-permute-start.8) | collective-permute-done | bytes 73760 | tf_op jit(solution)/shard_map/ppermute | solution.py:314
  37.4 0.1 collective-permute-start.11
  37.5 0.2 collective-permute-start.10
  37.6 2.5 %collective-permute-start.9 = (f32[144,128]{1,0:T(8,128)S(1)}, f32[144,128]{1,0:T(8,128)S(1)}, u32[]{:S(2)}, u32[]{:S(2)}) collective-permute-start(f32[144,128]{1,0:T(8,128)S(1)} %add.78), channel_id=1, source_target_pairs={{0,64},{1,65},{2,66},{3,67},{4,68},{5,69},{6,70},{7,71},{8,72},{9,... | collective-permute-start | bytes 221192 | tf_op jit(solution)/shard_map/ppermute | solution.py:464
  40.1 2.2 %collective-permute-done.11 = f32[144,128]{1,0:T(8,128)S(1)} collective-permute-done((f32[144,128]{1,0:T(8,128)S(1)}, f32[144,128]{1,0:T(8,128)S(1)}, u32[]{:S(2)}, u32[]{:S(2)}) %collective-permute-start.11) | collective-permute-done | bytes 73760 | tf_op jit(solution)/shard_map/ppermute | solution.py:464
  42.3 0.8 %collective-permute-done.10 = f32[144,128]{1,0:T(8,128)S(1)} collective-permute-done((f32[144,128]{1,0:T(8,128)S(1)}, f32[144,128]{1,0:T(8,128)S(1)}, u32[]{:S(2)}, u32[]{:S(2)}) %collective-permute-start.10) | collective-permute-done | bytes 73760 | tf_op jit(solution)/shard_map/ppermute | solution.py:464
  43.0 0.0 collective-permute-done.9
  43.1 0.6 collective-permute-start.14
  43.7 1.1 %collective-permute-start.13 = (f32[144,128]{1,0:T(8,128)S(1)}, f32[144,128]{1,0:T(8,128)S(1)}, u32[]{:S(2)}, u32[]{:S(2)}) collective-permute-start(f32[144,128]{1,0:T(8,128)S(1)} %add_add_fusion.1), channel_id=1, source_target_pairs={{0,24},{1,25},{2,26},{3,27},{4,28},{5,29},{6,30},{7,31},{8,16},{9,... | collective-permute-start | bytes 221192 | tf_op jit(solution)/shard_map/ppermute | solution.py:464
  44.7 1.1 %collective-permute-start.12 = (f32[144,128]{1,0:T(8,128)S(1)}, f32[144,128]{1,0:T(8,128)S(1)}, u32[]{:S(2)}, u32[]{:S(2)}) collective-permute-start(f32[144,128]{1,0:T(8,128)S(1)} %add_add_fusion.1), channel_id=1, source_target_pairs={{0,8},{1,9},{2,10},{3,11},{4,12},{5,13},{6,14},{7,15},{8,0},{9,1},... | collective-permute-start | bytes 221192 | tf_op jit(solution)/shard_map/ppermute | solution.py:464
  45.8 2.1 %collective-permute-done.14 = f32[144,128]{1,0:T(8,128)S(1)} collective-permute-done((f32[144,128]{1,0:T(8,128)S(1)}, f32[144,128]{1,0:T(8,128)S(1)}, u32[]{:S(2)}, u32[]{:S(2)}) %collective-permute-start.14) | collective-permute-done | bytes 73760 | tf_op jit(solution)/shard_map/ppermute | solution.py:464
  47.9 0.7 %collective-permute-done.13 = f32[144,128]{1,0:T(8,128)S(1)} collective-permute-done((f32[144,128]{1,0:T(8,128)S(1)}, f32[144,128]{1,0:T(8,128)S(1)}, u32[]{:S(2)}, u32[]{:S(2)}) %collective-permute-start.13) | collective-permute-done | bytes 73760 | tf_op jit(solution)/shard_map/ppermute | solution.py:464
  48.7 0.0 collective-permute-done.12
  48.7 0.1 collective-permute-start.15
  48.8 1.3 %update.1 = f32[96,1296]{1,0:T(8,128)} custom-call(f32[96,512]{1,0:T(8,128)S(1)} %get-tuple-element.98.back, bf16[512,1296]{1,0:T(8,128)(2,1)S(1)} %get-tuple-element.88.turned, f32[96,1296]{1,0:T(8,128)S(1)} %get-tuple-element.99.local), custom_call_target="tpu_custom_call" | custom-call | flops 254803968 | bytes 3000000 | tf_op jit(solution)/shard_map/update/pallas_call | solution.py:447
  50.1 2.8 %collective-permute-done.15 = f32[144,128]{1,0:T(8,128)S(1)} collective-permute-done((f32[144,128]{1,0:T(8,128)S(1)}, f32[144,128]{1,0:T(8,128)S(1)}, u32[]{:S(2)}, u32[]{:S(2)}) %collective-permute-start.15) | collective-permute-done | bytes 73760 | tf_op jit(solution)/shard_map/ppermute | solution.py:464
  52.9 0.1 collective-permute-start.17
  53.0 0.4 collective-permute-start.18
  53.3 4.4 %collective-permute-start.16 = (f32[144,128]{1,0:T(8,128)S(1)}, f32[144,128]{1,0:T(8,128)S(1)}, u32[]{:S(2)}, u32[]{:S(2)}) collective-permute-start(f32[144,128]{1,0:T(8,128)S(1)} %add.85), channel_id=1, source_target_pairs={{0,1},{1,0},{2,3},{3,2},{4,5},{5,4},{6,7},{7,6},{8,9},{9,8},{10,11... | collective-permute-start | bytes 221192 | tf_op jit(solution)/shard_map/ppermute | solution.py:464
  57.7 0.6 collective-permute-done.17
  58.3 0.1 collective-permute-done.18
  58.5 1.8 %collective-permute-done.16 = f32[144,128]{1,0:T(8,128)S(1)} collective-permute-done((f32[144,128]{1,0:T(8,128)S(1)}, f32[144,128]{1,0:T(8,128)S(1)}, u32[]{:S(2)}, u32[]{:S(2)}) %collective-permute-start.16) | collective-permute-done | bytes 73760 | tf_op jit(solution)/shard_map/ppermute | solution.py:464
  60.4 4.3 %collective-permute-start.19 = (f32[192,128]{1,0:T(8,128)S(1)}, f32[192,128]{1,0:T(8,128)S(1)}, u32[]{:S(2)}, u32[]{:S(2)}) collective-permute-start(f32[192,128]{1,0:T(8,128)S(1)} %pad_maximum_fusion.refs_0_), channel_id=1, source_target_pairs={{0,32},{32,0},{64,96},{96,64},{128,160},{160,128},{192,224},{224,1... | collective-permute-start | bytes 294920 | tf_op jit(solution)/shard_map/ppermute | solution.py:314
  64.7 0.9 %collective-permute-done.19.refs_1_ = f32[192,128]{1,0:T(8,128)S(1)} collective-permute-done((f32[192,128]{1,0:T(8,128)S(1)}, f32[192,128]{1,0:T(8,128)S(1)}, u32[]{:S(2)}, u32[]{:S(2)}) %collective-permute-start.19) | collective-permute-done | bytes 98336 | tf_op jit(solution)/shard_map/ppermute | solution.py:314
  65.6 1.1 %final.1 = f32[288,288]{1,0:T(8,128)} custom-call(s32[8,128]{1,0:T(8,128)S(1)} %add.71.odd, f32[192,128]{1,0:T(8,128)S(1)} %pad_maximum_fusion.refs_0_, f32[192,128]{1,0:T(8,128)S(1)} %collective-permute-done.19.refs_1_), custom_call_target="tpu_custom_call" | custom-call | flops 1000000 | bytes 700000 | tf_op jit(solution)/shard_map/final/pallas_call | solution.py:491
  (12 shorter events, 0.1 us)
Async XLA Ops:
  2.6 6.9 %collective-permute-start = (f32[96,128]{1,0:T(8,128)S(1)}, f32[96,128]{1,0:T(8,128)S(1)}, u32[]{:S(2)}, u32[]{:S(2)}) collective-permute-start(f32[96,128]{1,0:T(8,128)S(1)} %get-tuple-element.52), channel_id=1, source_target_pairs={{32,64},{96,128},{160,192},{224,0},{64,32},{128,96},{192,160},{0,2... | collective-permute-start | bytes 147464 | tf_op jit(solution)/shard_map/ppermute | solution.py:320
  5.3 4.1 %collective-permute-start.1 = (f32[96,128]{1,0:T(8,128)S(1)}, f32[96,128]{1,0:T(8,128)S(1)}, u32[]{:S(2)}, u32[]{:S(2)}) collective-permute-start(f32[96,128]{1,0:T(8,128)S(1)} %get-tuple-element.53), channel_id=1, source_target_pairs={{0,32},{32,0},{64,96},{96,64},{128,160},{160,128},{192,224},{224,1... | collective-permute-start | bytes 147464 | tf_op jit(solution)/shard_map/ppermute | solution.py:314
  9.5 10.8 %collective-permute-start.3 = (f32[96,128]{1,0:T(8,128)S(1)}, f32[96,128]{1,0:T(8,128)S(1)}, u32[]{:S(2)}, u32[]{:S(2)}) collective-permute-start(f32[96,128]{1,0:T(8,128)S(1)} %get-tuple-element.104), channel_id=1, source_target_pairs={{1,2},{3,4},{5,6},{7,8},{9,10},{11,12},{13,14},{15,16},{17,18},{19... | collective-permute-start | bytes 147464 | tf_op jit(solution)/shard_map/ppermute | solution.py:320
  17.4 3.0 %collective-permute-start.2 = (f32[96,128]{1,0:T(8,128)S(1)}, f32[96,128]{1,0:T(8,128)S(1)}, u32[]{:S(2)}, u32[]{:S(2)}) collective-permute-start(f32[96,128]{1,0:T(8,128)S(1)} %get-tuple-element.105), channel_id=1, source_target_pairs={{0,1},{1,0},{2,3},{3,2},{4,5},{5,4},{6,7},{7,6},{8,9},{9,8},{10,11... | collective-permute-start | bytes 147464 | tf_op jit(solution)/shard_map/ppermute | solution.py:314
  20.9 7.8 %collective-permute-start.4 = (f32[192,128]{1,0:T(8,128)S(1)}, f32[192,128]{1,0:T(8,128)S(1)}, u32[]{:S(2)}, u32[]{:S(2)}) collective-permute-start(f32[192,128]{1,0:T(8,128)S(1)} %get-tuple-element.75), channel_id=1, source_target_pairs={{0,1},{1,0},{2,3},{3,2},{4,5},{5,4},{6,7},{7,6},{8,9},{9,8},{10,11... | collective-permute-start | bytes 294920 | tf_op jit(solution)/shard_map/ppermute | solution.py:314
  22.5 6.3 %collective-permute-start.5 = (f32[96,128]{1,0:T(8,128)S(1)}, f32[96,128]{1,0:T(8,128)S(1)}, u32[]{:S(2)}, u32[]{:S(2)}) collective-permute-start(f32[96,128]{1,0:T(8,128)S(1)} %get-tuple-element.76), channel_id=1, source_target_pairs={{1,2},{3,4},{5,6},{7,8},{9,10},{11,12},{13,14},{15,16},{17,18},{19... | collective-permute-start | bytes 147464 | tf_op jit(solution)/shard_map/ppermute | solution.py:320
  28.8 4.3 %collective-permute-start.7 = (f32[96,128]{1,0:T(8,128)S(1)}, f32[96,128]{1,0:T(8,128)S(1)}, u32[]{:S(2)}, u32[]{:S(2)}) collective-permute-start(f32[96,128]{1,0:T(8,128)S(1)} %get-tuple-element.102), channel_id=1, source_target_pairs={{32,64},{96,128},{160,192},{224,0},{64,32},{128,96},{192,160},{0,2... | collective-permute-start | bytes 147464 | tf_op jit(solution)/shard_map/ppermute | solution.py:320
  31.3 1.8 %collective-permute-start.6 = (f32[96,128]{1,0:T(8,128)S(1)}, f32[96,128]{1,0:T(8,128)S(1)}, u32[]{:S(2)}, u32[]{:S(2)}) collective-permute-start(f32[96,128]{1,0:T(8,128)S(1)} %get-tuple-element.103), channel_id=1, source_target_pairs={{0,32},{32,0},{64,96},{96,64},{128,160},{160,128},{192,224},{224,1... | collective-permute-start | bytes 147464 | tf_op jit(solution)/shard_map/ppermute | solution.py:314
  33.8 3.5 %collective-permute-start.8 = (f32[144,128]{1,0:T(8,128)S(1)}, f32[144,128]{1,0:T(8,128)S(1)}, u32[]{:S(2)}, u32[]{:S(2)}) collective-permute-start(f32[144,128]{1,0:T(8,128)S(1)} %get-tuple-element.97), channel_id=1, source_target_pairs={{0,32},{32,0},{64,96},{96,64},{128,160},{160,128},{192,224},{224,1... | collective-permute-start | bytes 221192 | tf_op jit(solution)/shard_map/ppermute | solution.py:314
  37.4 4.9 %collective-permute-start.11 = (f32[144,128]{1,0:T(8,128)S(1)}, f32[144,128]{1,0:T(8,128)S(1)}, u32[]{:S(2)}, u32[]{:S(2)}) collective-permute-start(f32[144,128]{1,0:T(8,128)S(1)} %add.78), channel_id=1, source_target_pairs={{0,128},{1,129},{2,130},{3,131},{4,132},{5,133},{6,134},{7,135},{8... | collective-permute-start | bytes 221192 | tf_op jit(solution)/shard_map/ppermute | solution.py:464
  37.5 5.6 %collective-permute-start.10 = (f32[144,128]{1,0:T(8,128)S(1)}, f32[144,128]{1,0:T(8,128)S(1)}, u32[]{:S(2)}, u32[]{:S(2)}) collective-permute-start(f32[144,128]{1,0:T(8,128)S(1)} %add.78), channel_id=1, source_target_pairs={{0,192},{1,193},{2,194},{3,195},{4,196},{5,197},{6,198},{7,199},{8... | collective-permute-start | bytes 221192 | tf_op jit(solution)/shard_map/ppermute | solution.py:464
  37.6 5.4 %collective-permute-start.9 = (f32[144,128]{1,0:T(8,128)S(1)}, f32[144,128]{1,0:T(8,128)S(1)}, u32[]{:S(2)}, u32[]{:S(2)}) collective-permute-start(f32[144,128]{1,0:T(8,128)S(1)} %add.78), channel_id=1, source_target_pairs={{0,64},{1,65},{2,66},{3,67},{4,68},{5,69},{6,70},{7,71},{8,72},{9,... | collective-permute-start | bytes 221192 | tf_op jit(solution)/shard_map/ppermute | solution.py:464
  43.1 4.9 %collective-permute-start.14 = (f32[144,128]{1,0:T(8,128)S(1)}, f32[144,128]{1,0:T(8,128)S(1)}, u32[]{:S(2)}, u32[]{:S(2)}) collective-permute-start(f32[144,128]{1,0:T(8,128)S(1)} %add_add_fusion.1), channel_id=1, source_target_pairs={{0,16},{1,17},{2,18},{3,19},{4,20},{5,21},{6,22},{7,23},{8,24},{9,... | collective-permute-start | bytes 221192 | tf_op jit(solution)/shard_map/ppermute | solution.py:464
  43.7 5.0 %collective-permute-start.13 = (f32[144,128]{1,0:T(8,128)S(1)}, f32[144,128]{1,0:T(8,128)S(1)}, u32[]{:S(2)}, u32[]{:S(2)}) collective-permute-start(f32[144,128]{1,0:T(8,128)S(1)} %add_add_fusion.1), channel_id=1, source_target_pairs={{0,24},{1,25},{2,26},{3,27},{4,28},{5,29},{6,30},{7,31},{8,16},{9,... | collective-permute-start | bytes 221192 | tf_op jit(solution)/shard_map/ppermute | solution.py:464
  44.7 3.9 %collective-permute-start.12 = (f32[144,128]{1,0:T(8,128)S(1)}, f32[144,128]{1,0:T(8,128)S(1)}, u32[]{:S(2)}, u32[]{:S(2)}) collective-permute-start(f32[144,128]{1,0:T(8,128)S(1)} %add_add_fusion.1), channel_id=1, source_target_pairs={{0,8},{1,9},{2,10},{3,11},{4,12},{5,13},{6,14},{7,15},{8,0},{9,1},... | collective-permute-start | bytes 221192 | tf_op jit(solution)/shard_map/ppermute | solution.py:464
  48.7 4.2 %collective-permute-start.15 = (f32[144,128]{1,0:T(8,128)S(1)}, f32[144,128]{1,0:T(8,128)S(1)}, u32[]{:S(2)}, u32[]{:S(2)}) collective-permute-start(f32[144,128]{1,0:T(8,128)S(1)} %add_add_fusion), channel_id=1, source_target_pairs={{0,6},{1,7},{2,4},{3,5},{4,2},{5,3},{6,0},{7,1},{8,14},{9,15},{10,... | collective-permute-start | bytes 221192 | tf_op jit(solution)/shard_map/ppermute | solution.py:464
  52.9 5.5 %collective-permute-start.17 = (f32[144,128]{1,0:T(8,128)S(1)}, f32[144,128]{1,0:T(8,128)S(1)}, u32[]{:S(2)}, u32[]{:S(2)}) collective-permute-start(f32[144,128]{1,0:T(8,128)S(1)} %add.85), channel_id=1, source_target_pairs={{0,2},{1,3},{2,0},{3,1},{4,6},{5,7},{6,4},{7,5},{8,10},{9,11},{10,... | collective-permute-start | bytes 221192 | tf_op jit(solution)/shard_map/ppermute | solution.py:464
  53.0 5.5 %collective-permute-start.18 = (f32[144,128]{1,0:T(8,128)S(1)}, f32[144,128]{1,0:T(8,128)S(1)}, u32[]{:S(2)}, u32[]{:S(2)}) collective-permute-start(f32[144,128]{1,0:T(8,128)S(1)} %add.85), channel_id=1, source_target_pairs={{0,3},{1,2},{2,1},{3,0},{4,7},{5,6},{6,5},{7,4},{8,11},{9,10},{10,... | collective-permute-start | bytes 221192 | tf_op jit(solution)/shard_map/ppermute | solution.py:464
  53.3 7.0 %collective-permute-start.16 = (f32[144,128]{1,0:T(8,128)S(1)}, f32[144,128]{1,0:T(8,128)S(1)}, u32[]{:S(2)}, u32[]{:S(2)}) collective-permute-start(f32[144,128]{1,0:T(8,128)S(1)} %add.85), channel_id=1, source_target_pairs={{0,1},{1,0},{2,3},{3,2},{4,5},{5,4},{6,7},{7,6},{8,9},{9,8},{10,11... | collective-permute-start | bytes 221192 | tf_op jit(solution)/shard_map/ppermute | solution.py:464
  60.4 5.3 %collective-permute-start.19 = (f32[192,128]{1,0:T(8,128)S(1)}, f32[192,128]{1,0:T(8,128)S(1)}, u32[]{:S(2)}, u32[]{:S(2)}) collective-permute-start(f32[192,128]{1,0:T(8,128)S(1)} %pad_maximum_fusion.refs_0_), channel_id=1, source_target_pairs={{0,32},{32,0},{64,96},{96,64},{128,160},{160,128},{192,224},{224,1... | collective-permute-start | bytes 294920 | tf_op jit(solution)/shard_map/ppermute | solution.py:314

commit v2 on v1

--- a/solution.py
+++ b/solution.py
@@ -139,9 +139,9 @@
 
 
 def tail_kernel(
-    field, slab, factor, ritz_hbm, search_hbm, part, ph, plo, th, tlo, oh, olo, ritz, search, slab0, slab1, slab2, sem
+    field, slab, factor, ritz_hbm, search_hbm, part, ph, plo, th, tlo, oh, olo, ritz, search, slab0, slab1, sem
 ):
-    slabs = [(own_slab(factor, k), dest) for k, dest in enumerate((slab0, slab1, slab2))]
+    slabs = [(own_slab(factor, k), dest) for k, dest in enumerate((slab0, slab1))]
     copies = fetch([(ritz_hbm, ritz), (search_hbm, search)] + slabs, sem)
     place = halo_place()
     own = field.shape[1]
@@ -183,12 +183,13 @@
     out[:, :256] = out[:, :256] + slab_term(field, slab0)
 
 
-def last_kernel(field, slab2, slab3, head, factor, out, slab4, sem):
-    (copy,) = fetch([(own_slab(factor, 4), slab4)], sem)
+def last_kernel(field, slab3, head, factor, out, slab2, slab4, sem):
+    copies = fetch([(own_slab(factor, 2), slab2), (own_slab(factor, 4), slab4)], sem)
     out[:, :1024] = slab_term(field, slab3)
+    out[:, :512] = out[:, :512] + head[...]
+    copies[0].wait()
     out[:, :768] = out[:, :768] + slab_term(field, slab2)
-    out[:, :512] = out[:, :512] + head[...]
-    copy.wait()
+    copies[1].wait()
     term = slab_term(field, slab4)
     out[:, :1024] = out[:, :1024] + term[:, :1024]
     out[:, 1024:] = term[:, 1024:]
@@ -355,12 +356,12 @@
 
     placed, turned = shaped(320, 512, dtype=BF16), shaped(512, 320, dtype=BF16)
     wide = shaped(320, own, dtype=BF16)
-    part, ph, plo, th, tlo, oh, olo, ritz, search, slab0, slab1, slab2 = call(
+    part, ph, plo, th, tlo, oh, olo, ritz, search, slab0, slab1 = call(
         tail_kernel,
         (shaped(96, 320), placed, placed, turned, turned, wide, wide)
-        + (shaped(96, own), shaped(96, own), shaped(256, 256), shaped(256, 512), shaped(256, 768)),
+        + (shaped(96, own), shaped(96, own), shaped(256, 256), shaped(256, 512)),
         [VMEM, VMEM, HBM, HBM, HBM],
-        [pltpu.SemaphoreType.DMA((5,))],
+        [pltpu.SemaphoreType.DMA((4,))],
         flops=2 * 96 * 1296 * 320 * 3,
         moved=6000000,
         name="tail",
@@ -415,12 +416,12 @@
     own_part = call(
         last_kernel,
         shaped(96, TAIL),
-        [VMEM] * 4 + [HBM],
-        [pltpu.VMEM((256, TAIL), F32), pltpu.SemaphoreType.DMA((1,))],
+        [VMEM] * 3 + [HBM],
+        [pltpu.VMEM((256, 768), F32), pltpu.VMEM((256, TAIL), F32), pltpu.SemaphoreType.DMA((2,))],
         flops=2 * 2 * 96 * 256 * 256 * 12 * 3,
         moved=3000000,
         name="last",
-    )(field, slab2, slab3, head, factor)
+    )(field, slab3, head, factor)
     rya, ryb, own_part = lax.optimization_barrier((rya, ryb, own_part))
 
     relay = jnp.where(lane >= EDGE, rya[:96] + ryb, 0.0)
@@ -479,6 +480,7 @@
     three = swap_apart(total, (0, 3), (0, 7))
     two = swap_apart(total, (0, 2), (0, 6))
     one = swap_apart(total, (0, 1), (0, 1))
+    three, two, one = lax.optimization_barrier((three, two, one))
     late = (total[:96] + one[:96]) + (two[:96] + three[:96])
     mine = jnp.concatenate([late, total[96:] + two[96:], one[96:] + three[96:]], axis=0)
     other = swap(mine, "sx", 1)

time: 67.1 us -> 67.4 us (level)
  waiting for transfers between devices: 13.9 us -> 15.1 us
    ppermute x10, waiting for transfers between devices: 11.2 us -> 12.5 us  [swap_apart(): return lax.ppermute(value, ('sx', 'sy'), route)]
    ppermute x10, starting transfers between devices: 10.4 us -> 9.49 us  [swap_apart(): return lax.ppermute(value, ('sx', 'sy'), route)]
  transfers between devices with their start and end apart: 20 -> 20, of which waited for: 11 -> 10; matrix products, arithmetic and copies ran while one was open for 0% -> 0% of each run, Pallas kernels for 18% -> 17%
where the time goes in v2:
time: 67.4 us; the launch traced here: 67.2 us
  starting transfers between devices  35.1 us (52%)
  Pallas kernels  15.8 us (23%)
  waiting for transfers between devices  15.1 us (22%)
  between operations  0.99 us (1%)
    ppermute x4, starting transfers between devices, swap_odd(): return lax.ppermute(block, axis, route + [(b, a) for a, b in route])  15.5 us
    ppermute x10, waiting for transfers between devices, swap_apart(): return lax.ppermute(value, ('sx', 'sy'), route)  12.5 us
    ppermute x6, starting transfers between devices, swap(): lax.ppermute(block, axis, [(i, i ^ step) for i in range(lax.axis_size(axi...  10.1 us
    ppermute x10, starting transfers between devices, swap_apart(): return lax.ppermute(value, ('sx', 'sy'), route)  9.49 us
    pallas_call x1, Pallas kernels, body(): call(last_kernel, shaped(96, TAIL), [VMEM] * 3 + [HBM], [pltpu.VMEM((256,...  3.23 us
    pallas_call x1, Pallas kernels, body(): call(tail_kernel, (shaped(96, 320), placed, placed, turned, turned, wide,...  2.25 us
    pallas_call x1, Pallas kernels, body(): call(side_kernel, (msg, msg, shaped(512, own, dtype=BF16), shaped(512, 51...  1.98 us
    ppermute x6, waiting for transfers between devices, swap(): lax.ppermute(block, axis, [(i, i ^ step) for i in range(lax.axis_size(axi...  1.87 us
  transfers between devices with their start and end apart: 20, of which 10 were waited for; matrix products, arithmetic and copies ran while one was open for 0% of the time, Pallas kernels for 17%

profile of v2, /device:TPU:1, one launch (start us, length us, event | category | flops | bytes accessed | tf_op | source)
XLA Modules:
  0.0 67.2 jit_solution(9652718309734582199)
XLA Ops:
  0.7 0.1 add.71.odd
  0.7 1.8 %gather.1 = (f32[96,128]{1,0:T(8,128)S(1)}, f32[96,128]{1,0:T(8,128)S(1)}, f32[96,128]{1,0:T(8,128)S(1)}, f32[96,128]{1,0:T(8,128)S(1)}, bf16[192,1296]{1,0:T(8,...) custom-call(s32[8,128]{1,0:T(8,128)S(1)} %add.71.odd, s32[1,1,8]{2,1,0:T(1,128)} %count_hbm.1, ...), custom_call_target="tpu_custom_call" | custom-call | flops 254803968 | bytes 2000000 | tf_op jit(solution)/shard_map/gather/pallas_call | solution.py:332
  2.6 2.8 %collective-permute-start = (f32[96,128]{1,0:T(8,128)S(1)}, f32[96,128]{1,0:T(8,128)S(1)}, u32[]{:S(2)}, u32[]{:S(2)}) collective-permute-start(f32[96,128]{1,0:T(8,128)S(1)} %get-tuple-element.54), channel_id=1, source_target_pairs={{32,64},{96,128},{160,192},{224,0},{64,32},{128,96},{192,160},{0,2... | collective-permute-start | bytes 147464 | tf_op jit(solution)/shard_map/ppermute | solution.py:321
  5.3 1.3 %collective-permute-start.1 = (f32[96,128]{1,0:T(8,128)S(1)}, f32[96,128]{1,0:T(8,128)S(1)}, u32[]{:S(2)}, u32[]{:S(2)}) collective-permute-start(f32[96,128]{1,0:T(8,128)S(1)} %get-tuple-element.55), channel_id=1, source_target_pairs={{0,32},{32,0},{64,96},{96,64},{128,160},{160,128},{192,224},{224,1... | collective-permute-start | bytes 147464 | tf_op jit(solution)/shard_map/ppermute | solution.py:315
  6.6 2.3 %tail.1 = (f32[96,320]{1,0:T(8,128)S(1)}, bf16[320,512]{1,0:T(8,128)(2,1)S(1)}, bf16[320,512]{1,0:T(8,128)(2,1)S(1)}, bf16[512,320]{1,0:T(8,128)(2,1)S(1)}, bf16...) custom-call(bf16[192,1296]{1,0:T(8,128)(2,1)S(1)} %get-tuple-element, ...), custom_call_target="tpu_custom_call" | custom-call | flops 238878720 | bytes 6000000 | tf_op jit(solution)/shard_map/tail/pallas_call | solution.py:359
  8.9 0.0 collective-permute-done.sxb
  8.9 0.0 collective-permute-done.1.sxa
  8.9 7.9 %collective-permute-start.3 = (f32[96,128]{1,0:T(8,128)S(1)}, f32[96,128]{1,0:T(8,128)S(1)}, u32[]{:S(2)}, u32[]{:S(2)}) collective-permute-start(f32[96,128]{1,0:T(8,128)S(1)} %get-tuple-element.108), channel_id=1, source_target_pairs={{1,2},{3,4},{5,6},{7,8},{9,10},{11,12},{13,14},{15,16},{17,18},{19... | collective-permute-start | bytes 147464 | tf_op jit(solution)/shard_map/ppermute | solution.py:321
  16.8 0.0 collective-permute-start.2
  16.8 0.9 %head.1 = f32[96,512]{1,0:T(8,128)S(1)} custom-call(bf16[192,1296]{1,0:T(8,128)(2,1)S(1)} %get-tuple-element.56.field, f32[256,256]{1,0:T(8,128)S(1)} %get-tuple-element.63.slab0, f32[256,512]{1,0:T(8,128)S(1)} %get-tuple-element.64.slab1), custom_call_target="tpu_custom_call" | custom-call | flops 226492416 | bytes 1200000 | tf_op jit(solution)/shard_map/head/pallas_call | solution.py:395
  17.7 2.0 %side.1 = (f32[96,128]{1,0:T(8,128)S(1)}, f32[96,128]{1,0:T(8,128)S(1)}, bf16[512,1296]{1,0:T(8,128)(2,1)S(1)}, bf16[512,512]{1,0:T(8,128)(2,1)S(1)}, bf16[256,1...) custom-call(s32[8,128]{1,0:T(8,128)S(1)} %add.71.odd, ...), custom_call_target="tpu_custom_call" | custom-call | flops 382205952 | bytes 3000000 | tf_op jit(solution)/shard_map/side/pallas_call | solution.py:375
  19.7 0.0 collective-permute-done.3.syb
  19.7 0.0 collective-permute-done.2.sya
  19.8 0.6 halo.1
  20.4 1.5 %collective-permute-start.4 = (f32[192,128]{1,0:T(8,128)S(1)}, f32[192,128]{1,0:T(8,128)S(1)}, u32[]{:S(2)}, u32[]{:S(2)}) collective-permute-start(f32[192,128]{1,0:T(8,128)S(1)} %get-tuple-element.77), channel_id=1, source_target_pairs={{0,1},{1,0},{2,3},{3,2},{4,5},{5,4},{6,7},{7,6},{8,9},{9,8},{10,11... | collective-permute-start | bytes 294920 | tf_op jit(solution)/shard_map/ppermute | solution.py:315
  21.9 2.4 %collective-permute-start.5 = (f32[96,128]{1,0:T(8,128)S(1)}, f32[96,128]{1,0:T(8,128)S(1)}, u32[]{:S(2)}, u32[]{:S(2)}) collective-permute-start(f32[96,128]{1,0:T(8,128)S(1)} %get-tuple-element.78), channel_id=1, source_target_pairs={{1,2},{3,4},{5,6},{7,8},{9,10},{11,12},{13,14},{15,16},{17,18},{19... | collective-permute-start | bytes 147464 | tf_op jit(solution)/shard_map/ppermute | solution.py:321
  24.3 3.2 %last.1.own_part = f32[96,1280]{1,0:T(8,128)S(1)} custom-call(bf16[192,1296]{1,0:T(8,128)(2,1)S(1)} %get-tuple-element.56.field, f32[256,1024]{1,0:T(8,128)S(1)} %get-tuple-element.79.slab3, f32[96,512]{1,0:T(8,128)S(1)} %head.1, f32[1,1,1600,1600]{3,2,1,0:T(8,128)} %factor.7), custom_call_target="tpu_custom_call" | custom-call | flops 905969664 | bytes 3000000 | tf_op jit(solution)/shard_map/last/pallas_call | solution.py:416
  27.5 0.7 collective-permute-done.5.ryb
  28.2 0.0 collective-permute-done.4.rya
  28.2 2.5 %collective-permute-start.7 = (f32[96,128]{1,0:T(8,128)S(1)}, f32[96,128]{1,0:T(8,128)S(1)}, u32[]{:S(2)}, u32[]{:S(2)}) collective-permute-start(f32[96,128]{1,0:T(8,128)S(1)} %get-tuple-element.106), channel_id=1, source_target_pairs={{32,64},{96,128},{160,192},{224,0},{64,32},{128,96},{192,160},{0,2... | collective-permute-start | bytes 147464 | tf_op jit(solution)/shard_map/ppermute | solution.py:321
  30.7 0.0 collective-permute-start.6
  30.7 1.8 %local.1 = (f32[96,1296]{1,0:T(8,128)S(1)}, f32[96,512]{1,0:T(8,128)S(1)}, f32[288,96]{1,0:T(8,128)S(1)}) custom-call(f32[96,1280]{1,0:T(8,128)S(1)} %last.1.own_part, f32[96,320]{1,0:T(8,128)S(1)} %get-tuple-element.86.half, bf16[320,1296]{1,0:T(8,128)(2,1)S(1)} %get-tuple-element.87.oh, bf16[320,1296]{1,0:T(8,128)(2,1)S(1)} %get-tuple-element.88.olo, ...), custom_call_target="tpu_custom_call" | custom-call | flops 821145600 | bytes 4000000 | tf_op jit(solution)/shard_map/local/pallas_call | solution.py:430
  32.5 0.0 collective-permute-done.7.rxb
  32.5 0.0 collective-permute-done.6.rxa
  32.5 0.8 %gram.1 = (f32[144,128]{1,0:T(8,128)S(1)}, f32[144,128]{1,0:T(8,128)S(1)}, f32[96,512]{1,0:T(8,128)S(1)}) custom-call(s32[8,128]{1,0:T(8,128)S(1)} %add.71.odd, f32[96,128]{1,0:T(8,128)S(1)} %collective-permute-done.6.rxa, f32[96,128]{1,0:T(8,128)S(1)} %collective-permute-done.7.rxb, f32[192,128]{1,0:T(8,128)S(1)} %collective-permute-done.4.rya, ...), custom_call_target="tpu_custom_call" | custom-call | flops 265420800 | bytes 2000000 | tf_op jit(solution)/shard_map/gram/pallas_call | solution.py:439
  33.3 2.6 %collective-permute-start.8 = (f32[144,128]{1,0:T(8,128)S(1)}, f32[144,128]{1,0:T(8,128)S(1)}, u32[]{:S(2)}, u32[]{:S(2)}) collective-permute-start(f32[144,128]{1,0:T(8,128)S(1)} %get-tuple-element.98), channel_id=1, source_target_pairs={{0,32},{32,0},{64,96},{96,64},{128,160},{160,128},{192,224},{224,1... | collective-permute-start | bytes 221192 | tf_op jit(solution)/shard_map/ppermute | solution.py:315
  35.9 0.9 %collective-permute-done.8 = f32[144,128]{1,0:T(8,128)S(1)} collective-permute-done((f32[144,128]{1,0:T(8,128)S(1)}, f32[144,128]{1,0:T(8,128)S(1)}, u32[]{:S(2)}, u32[]{:S(2)}) %collective-permute-start.8) | collective-permute-done | bytes 73760 | tf_op jit(solution)/shard_map/ppermute | solution.py:315
  36.8 0.1 collective-permute-start.11
  36.9 0.2 collective-permute-start.10
  37.1 2.5 %collective-permute-start.9 = (f32[144,128]{1,0:T(8,128)S(1)}, f32[144,128]{1,0:T(8,128)S(1)}, u32[]{:S(2)}, u32[]{:S(2)}) collective-permute-start(f32[144,128]{1,0:T(8,128)S(1)} %add.78), channel_id=1, source_target_pairs={{0,64},{1,65},{2,66},{3,67},{4,68},{5,69},{6,70},{7,71},{8,72},{9,... | collective-permute-start | bytes 221192 | tf_op jit(solution)/shard_map/ppermute | solution.py:465
  39.5 2.2 %collective-permute-done.11 = f32[144,128]{1,0:T(8,128)S(1)} collective-permute-done((f32[144,128]{1,0:T(8,128)S(1)}, f32[144,128]{1,0:T(8,128)S(1)}, u32[]{:S(2)}, u32[]{:S(2)}) %collective-permute-start.11) | collective-permute-done | bytes 73760 | tf_op jit(solution)/shard_map/ppermute | solution.py:465
  41.7 0.8 %collective-permute-done.10 = f32[144,128]{1,0:T(8,128)S(1)} collective-permute-done((f32[144,128]{1,0:T(8,128)S(1)}, f32[144,128]{1,0:T(8,128)S(1)}, u32[]{:S(2)}, u32[]{:S(2)}) %collective-permute-start.10) | collective-permute-done | bytes 73760 | tf_op jit(solution)/shard_map/ppermute | solution.py:465
  42.5 0.0 collective-permute-done.9
  42.5 0.6 collective-permute-start.14
  43.1 1.1 %collective-permute-start.13 = (f32[144,128]{1,0:T(8,128)S(1)}, f32[144,128]{1,0:T(8,128)S(1)}, u32[]{:S(2)}, u32[]{:S(2)}) collective-permute-start(f32[144,128]{1,0:T(8,128)S(1)} %add_add_fusion.1), channel_id=1, source_target_pairs={{0,24},{1,25},{2,26},{3,27},{4,28},{5,29},{6,30},{7,31},{8,16},{9,... | collective-permute-start | bytes 221192 | tf_op jit(solution)/shard_map/ppermute | solution.py:465
  44.2 1.1 %collective-permute-start.12 = (f32[144,128]{1,0:T(8,128)S(1)}, f32[144,128]{1,0:T(8,128)S(1)}, u32[]{:S(2)}, u32[]{:S(2)}) collective-permute-start(f32[144,128]{1,0:T(8,128)S(1)} %add_add_fusion.1), channel_id=1, source_target_pairs={{0,8},{1,9},{2,10},{3,11},{4,12},{5,13},{6,14},{7,15},{8,0},{9,1},... | collective-permute-start | bytes 221192 | tf_op jit(solution)/shard_map/ppermute | solution.py:465
  45.2 2.1 %collective-permute-done.14 = f32[144,128]{1,0:T(8,128)S(1)} collective-permute-done((f32[144,128]{1,0:T(8,128)S(1)}, f32[144,128]{1,0:T(8,128)S(1)}, u32[]{:S(2)}, u32[]{:S(2)}) %collective-permute-start.14) | collective-permute-done | bytes 73760 | tf_op jit(solution)/shard_map/ppermute | solution.py:465
  47.4 0.7 %collective-permute-done.13 = f32[144,128]{1,0:T(8,128)S(1)} collective-permute-done((f32[144,128]{1,0:T(8,128)S(1)}, f32[144,128]{1,0:T(8,128)S(1)}, u32[]{:S(2)}, u32[]{:S(2)}) %collective-permute-start.13) | collective-permute-done | bytes 73760 | tf_op jit(solution)/shard_map/ppermute | solution.py:465
  48.1 0.0 collective-permute-done.12
  48.1 0.1 collective-permute-start.15
  48.2 1.3 %update.1 = f32[96,1296]{1,0:T(8,128)} custom-call(f32[96,512]{1,0:T(8,128)S(1)} %get-tuple-element.99.back, bf16[512,1296]{1,0:T(8,128)(2,1)S(1)} %get-tuple-element.89.turned, f32[96,1296]{1,0:T(8,128)S(1)} %get-tuple-element.100.local), custom_call_target="tpu_custom_call" | custom-call | flops 254803968 | bytes 3000000 | tf_op jit(solution)/shard_map/update/pallas_call | solution.py:448
  49.5 2.8 %collective-permute-done.15 = f32[144,128]{1,0:T(8,128)S(1)} collective-permute-done((f32[144,128]{1,0:T(8,128)S(1)}, f32[144,128]{1,0:T(8,128)S(1)}, u32[]{:S(2)}, u32[]{:S(2)}) %collective-permute-start.15) | collective-permute-done | bytes 73760 | tf_op jit(solution)/shard_map/ppermute | solution.py:465
  52.3 0.1 collective-permute-start.18
  52.4 1.4 %collective-permute-start.17 = (f32[144,128]{1,0:T(8,128)S(1)}, f32[144,128]{1,0:T(8,128)S(1)}, u32[]{:S(2)}, u32[]{:S(2)}) collective-permute-start(f32[144,128]{1,0:T(8,128)S(1)} %add.85), channel_id=1, source_target_pairs={{0,2},{1,3},{2,0},{3,1},{4,6},{5,7},{6,4},{7,5},{8,10},{9,11},{10,... | collective-permute-start | bytes 221192 | tf_op jit(solution)/shard_map/ppermute | solution.py:465
  53.9 2.4 %collective-permute-start.16 = (f32[144,128]{1,0:T(8,128)S(1)}, f32[144,128]{1,0:T(8,128)S(1)}, u32[]{:S(2)}, u32[]{:S(2)}) collective-permute-start(f32[144,128]{1,0:T(8,128)S(1)} %add.85), channel_id=1, source_target_pairs={{0,3},{1,2},{2,1},{3,0},{4,7},{5,6},{6,5},{7,4},{8,11},{9,10},{10,... | collective-permute-start | bytes 221192 | tf_op jit(solution)/shard_map/ppermute | solution.py:465
  56.3 0.0 collective-permute-done.18
  56.3 1.6 %collective-permute-done.17 = f32[144,128]{1,0:T(8,128)S(1)} collective-permute-done((f32[144,128]{1,0:T(8,128)S(1)}, f32[144,128]{1,0:T(8,128)S(1)}, u32[]{:S(2)}, u32[]{:S(2)}) %collective-permute-start.17) | collective-permute-done | bytes 73760 | tf_op jit(solution)/shard_map/ppermute | solution.py:465
  57.9 2.3 %collective-permute-done.16 = f32[144,128]{1,0:T(8,128)S(1)} collective-permute-done((f32[144,128]{1,0:T(8,128)S(1)}, f32[144,128]{1,0:T(8,128)S(1)}, u32[]{:S(2)}, u32[]{:S(2)}) %collective-permute-start.16) | collective-permute-done | bytes 73760 | tf_op jit(solution)/shard_map/ppermute | solution.py:465
  60.2 4.7 %collective-permute-start.19 = (f32[192,128]{1,0:T(8,128)S(1)}, f32[192,128]{1,0:T(8,128)S(1)}, u32[]{:S(2)}, u32[]{:S(2)}) collective-permute-start(f32[192,128]{1,0:T(8,128)S(1)} %pad_maximum_fusion.refs_0_), channel_id=1, source_target_pairs={{0,32},{32,0},{64,96},{96,64},{128,160},{160,128},{192,224},{224,1... | collective-permute-start | bytes 294920 | tf_op jit(solution)/shard_map/ppermute | solution.py:315
  64.9 0.9 %collective-permute-done.19.refs_1_ = f32[192,128]{1,0:T(8,128)S(1)} collective-permute-done((f32[192,128]{1,0:T(8,128)S(1)}, f32[192,128]{1,0:T(8,128)S(1)}, u32[]{:S(2)}, u32[]{:S(2)}) %collective-permute-start.19) | collective-permute-done | bytes 98336 | tf_op jit(solution)/shard_map/ppermute | solution.py:315
  65.9 1.1 %final.1 = f32[288,288]{1,0:T(8,128)} custom-call(s32[8,128]{1,0:T(8,128)S(1)} %add.71.odd, f32[192,128]{1,0:T(8,128)S(1)} %pad_maximum_fusion.refs_0_, f32[192,128]{1,0:T(8,128)S(1)} %collective-permute-done.19.refs_1_), custom_call_target="tpu_custom_call" | custom-call | flops 1000000 | bytes 700000 | tf_op jit(solution)/shard_map/final/pallas_call | solution.py:493
  (11 shorter events, 0.1 us)
Async XLA Ops:
  2.6 6.3 %collective-permute-start = (f32[96,128]{1,0:T(8,128)S(1)}, f32[96,128]{1,0:T(8,128)S(1)}, u32[]{:S(2)}, u32[]{:S(2)}) collective-permute-start(f32[96,128]{1,0:T(8,128)S(1)} %get-tuple-element.54), channel_id=1, source_target_pairs={{32,64},{96,128},{160,192},{224,0},{64,32},{128,96},{192,160},{0,2... | collective-permute-start | bytes 147464 | tf_op jit(solution)/shard_map/ppermute | solution.py:321
  5.3 3.6 %collective-permute-start.1 = (f32[96,128]{1,0:T(8,128)S(1)}, f32[96,128]{1,0:T(8,128)S(1)}, u32[]{:S(2)}, u32[]{:S(2)}) collective-permute-start(f32[96,128]{1,0:T(8,128)S(1)} %get-tuple-element.55), channel_id=1, source_target_pairs={{0,32},{32,0},{64,96},{96,64},{128,160},{160,128},{192,224},{224,1... | collective-permute-start | bytes 147464 | tf_op jit(solution)/shard_map/ppermute | solution.py:315
  8.9 10.8 %collective-permute-start.3 = (f32[96,128]{1,0:T(8,128)S(1)}, f32[96,128]{1,0:T(8,128)S(1)}, u32[]{:S(2)}, u32[]{:S(2)}) collective-permute-start(f32[96,128]{1,0:T(8,128)S(1)} %get-tuple-element.108), channel_id=1, source_target_pairs={{1,2},{3,4},{5,6},{7,8},{9,10},{11,12},{13,14},{15,16},{17,18},{19... | collective-permute-start | bytes 147464 | tf_op jit(solution)/shard_map/ppermute | solution.py:321
  16.8 3.0 %collective-permute-start.2 = (f32[96,128]{1,0:T(8,128)S(1)}, f32[96,128]{1,0:T(8,128)S(1)}, u32[]{:S(2)}, u32[]{:S(2)}) collective-permute-start(f32[96,128]{1,0:T(8,128)S(1)} %get-tuple-element.109), channel_id=1, source_target_pairs={{0,1},{1,0},{2,3},{3,2},{4,5},{5,4},{6,7},{7,6},{8,9},{9,8},{10,11... | collective-permute-start | bytes 147464 | tf_op jit(solution)/shard_map/ppermute | solution.py:315
  20.4 7.8 %collective-permute-start.4 = (f32[192,128]{1,0:T(8,128)S(1)}, f32[192,128]{1,0:T(8,128)S(1)}, u32[]{:S(2)}, u32[]{:S(2)}) collective-permute-start(f32[192,128]{1,0:T(8,128)S(1)} %get-tuple-element.77), channel_id=1, source_target_pairs={{0,1},{1,0},{2,3},{3,2},{4,5},{5,4},{6,7},{7,6},{8,9},{9,8},{10,11... | collective-permute-start | bytes 294920 | tf_op jit(solution)/shard_map/ppermute | solution.py:315
  21.9 6.3 %collective-permute-start.5 = (f32[96,128]{1,0:T(8,128)S(1)}, f32[96,128]{1,0:T(8,128)S(1)}, u32[]{:S(2)}, u32[]{:S(2)}) collective-permute-start(f32[96,128]{1,0:T(8,128)S(1)} %get-tuple-element.78), channel_id=1, source_target_pairs={{1,2},{3,4},{5,6},{7,8},{9,10},{11,12},{13,14},{15,16},{17,18},{19... | collective-permute-start | bytes 147464 | tf_op jit(solution)/shard_map/ppermute | solution.py:321
  28.2 4.3 %collective-permute-start.7 = (f32[96,128]{1,0:T(8,128)S(1)}, f32[96,128]{1,0:T(8,128)S(1)}, u32[]{:S(2)}, u32[]{:S(2)}) collective-permute-start(f32[96,128]{1,0:T(8,128)S(1)} %get-tuple-element.106), channel_id=1, source_target_pairs={{32,64},{96,128},{160,192},{224,0},{64,32},{128,96},{192,160},{0,2... | collective-permute-start | bytes 147464 | tf_op jit(solution)/shard_map/ppermute | solution.py:321
  30.7 1.8 %collective-permute-start.6 = (f32[96,128]{1,0:T(8,128)S(1)}, f32[96,128]{1,0:T(8,128)S(1)}, u32[]{:S(2)}, u32[]{:S(2)}) collective-permute-start(f32[96,128]{1,0:T(8,128)S(1)} %get-tuple-element.107), channel_id=1, source_target_pairs={{0,32},{32,0},{64,96},{96,64},{128,160},{160,128},{192,224},{224,1... | collective-permute-start | bytes 147464 | tf_op jit(solution)/shard_map/ppermute | solution.py:315
  33.3 3.5 %collective-permute-start.8 = (f32[144,128]{1,0:T(8,128)S(1)}, f32[144,128]{1,0:T(8,128)S(1)}, u32[]{:S(2)}, u32[]{:S(2)}) collective-permute-start(f32[144,128]{1,0:T(8,128)S(1)} %get-tuple-element.98), channel_id=1, source_target_pairs={{0,32},{32,0},{64,96},{96,64},{128,160},{160,128},{192,224},{224,1... | collective-permute-start | bytes 221192 | tf_op jit(solution)/shard_map/ppermute | solution.py:315
  36.8 4.9 %collective-permute-start.11 = (f32[144,128]{1,0:T(8,128)S(1)}, f32[144,128]{1,0:T(8,128)S(1)}, u32[]{:S(2)}, u32[]{:S(2)}) collective-permute-start(f32[144,128]{1,0:T(8,128)S(1)} %add.78), channel_id=1, source_target_pairs={{0,128},{1,129},{2,130},{3,131},{4,132},{5,133},{6,134},{7,135},{8... | collective-permute-start | bytes 221192 | tf_op jit(solution)/shard_map/ppermute | solution.py:465
  36.9 5.6 %collective-permute-start.10 = (f32[144,128]{1,0:T(8,128)S(1)}, f32[144,128]{1,0:T(8,128)S(1)}, u32[]{:S(2)}, u32[]{:S(2)}) collective-permute-start(f32[144,128]{1,0:T(8,128)S(1)} %add.78), channel_id=1, source_target_pairs={{0,192},{1,193},{2,194},{3,195},{4,196},{5,197},{6,198},{7,199},{8... | collective-permute-start | bytes 221192 | tf_op jit(solution)/shard_map/ppermute | solution.py:465
  37.1 5.4 %collective-permute-start.9 = (f32[144,128]{1,0:T(8,128)S(1)}, f32[144,128]{1,0:T(8,128)S(1)}, u32[]{:S(2)}, u32[]{:S(2)}) collective-permute-start(f32[144,128]{1,0:T(8,128)S(1)} %add.78), channel_id=1, source_target_pairs={{0,64},{1,65},{2,66},{3,67},{4,68},{5,69},{6,70},{7,71},{8,72},{9,... | collective-permute-start | bytes 221192 | tf_op jit(solution)/shard_map/ppermute | solution.py:465
  42.5 4.9 %collective-permute-start.14 = (f32[144,128]{1,0:T(8,128)S(1)}, f32[144,128]{1,0:T(8,128)S(1)}, u32[]{:S(2)}, u32[]{:S(2)}) collective-permute-start(f32[144,128]{1,0:T(8,128)S(1)} %add_add_fusion.1), channel_id=1, source_target_pairs={{0,16},{1,17},{2,18},{3,19},{4,20},{5,21},{6,22},{7,23},{8,24},{9,... | collective-permute-start | bytes 221192 | tf_op jit(solution)/shard_map/ppermute | solution.py:465
  43.1 5.0 %collective-permute-start.13 = (f32[144,128]{1,0:T(8,128)S(1)}, f32[144,128]{1,0:T(8,128)S(1)}, u32[]{:S(2)}, u32[]{:S(2)}) collective-permute-start(f32[144,128]{1,0:T(8,128)S(1)} %add_add_fusion.1), channel_id=1, source_target_pairs={{0,24},{1,25},{2,26},{3,27},{4,28},{5,29},{6,30},{7,31},{8,16},{9,... | collective-permute-start | bytes 221192 | tf_op jit(solution)/shard_map/ppermute | solution.py:465
  44.2 3.9 %collective-permute-start.12 = (f32[144,128]{1,0:T(8,128)S(1)}, f32[144,128]{1,0:T(8,128)S(1)}, u32[]{:S(2)}, u32[]{:S(2)}) collective-permute-start(f32[144,128]{1,0:T(8,128)S(1)} %add_add_fusion.1), channel_id=1, source_target_pairs={{0,8},{1,9},{2,10},{3,11},{4,12},{5,13},{6,14},{7,15},{8,0},{9,1},... | collective-permute-start | bytes 221192 | tf_op jit(solution)/shard_map/ppermute | solution.py:465
  48.1 4.2 %collective-permute-start.15 = (f32[144,128]{1,0:T(8,128)S(1)}, f32[144,128]{1,0:T(8,128)S(1)}, u32[]{:S(2)}, u32[]{:S(2)}) collective-permute-start(f32[144,128]{1,0:T(8,128)S(1)} %add_add_fusion), channel_id=1, source_target_pairs={{0,6},{1,7},{2,4},{3,5},{4,2},{5,3},{6,0},{7,1},{8,14},{9,15},{10,... | collective-permute-start | bytes 221192 | tf_op jit(solution)/shard_map/ppermute | solution.py:465
  52.3 4.0 %collective-permute-start.18 = (f32[144,128]{1,0:T(8,128)S(1)}, f32[144,128]{1,0:T(8,128)S(1)}, u32[]{:S(2)}, u32[]{:S(2)}) collective-permute-start(f32[144,128]{1,0:T(8,128)S(1)} %add.85), channel_id=1, source_target_pairs={{0,1},{1,0},{2,3},{3,2},{4,5},{5,4},{6,7},{7,6},{8,9},{9,8},{10,11... | collective-permute-start | bytes 221192 | tf_op jit(solution)/shard_map/ppermute | solution.py:465
  52.4 5.5 %collective-permute-start.17 = (f32[144,128]{1,0:T(8,128)S(1)}, f32[144,128]{1,0:T(8,128)S(1)}, u32[]{:S(2)}, u32[]{:S(2)}) collective-permute-start(f32[144,128]{1,0:T(8,128)S(1)} %add.85), channel_id=1, source_target_pairs={{0,2},{1,3},{2,0},{3,1},{4,6},{5,7},{6,4},{7,5},{8,10},{9,11},{10,... | collective-permute-start | bytes 221192 | tf_op jit(solution)/shard_map/ppermute | solution.py:465
  53.9 6.3 %collective-permute-start.16 = (f32[144,128]{1,0:T(8,128)S(1)}, f32[144,128]{1,0:T(8,128)S(1)}, u32[]{:S(2)}, u32[]{:S(2)}) collective-permute-start(f32[144,128]{1,0:T(8,128)S(1)} %add.85), channel_id=1, source_target_pairs={{0,3},{1,2},{2,1},{3,0},{4,7},{5,6},{6,5},{7,4},{8,11},{9,10},{10,... | collective-permute-start | bytes 221192 | tf_op jit(solution)/shard_map/ppermute | solution.py:465
  60.2 5.6 %collective-permute-start.19 = (f32[192,128]{1,0:T(8,128)S(1)}, f32[192,128]{1,0:T(8,128)S(1)}, u32[]{:S(2)}, u32[]{:S(2)}) collective-permute-start(f32[192,128]{1,0:T(8,128)S(1)} %pad_maximum_fusion.refs_0_), channel_id=1, source_target_pairs={{0,32},{32,0},{64,96},{96,64},{128,160},{160,128},{192,224},{224,1... | collective-permute-start | bytes 294920 | tf_op jit(solution)/shard_map/ppermute | solution.py:315

commit v3 on v2

--- a/solution.py
+++ b/solution.py
@@ -480,7 +480,6 @@
     three = swap_apart(total, (0, 3), (0, 7))
     two = swap_apart(total, (0, 2), (0, 6))
     one = swap_apart(total, (0, 1), (0, 1))
-    three, two, one = lax.optimization_barrier((three, two, one))
     late = (total[:96] + one[:96]) + (two[:96] + three[:96])
     mine = jnp.concatenate([late, total[96:] + two[96:], one[96:] + three[96:]], axis=0)
     other = swap(mine, "sx", 1)

time: 67.4 us -> 66.5 us (0.987)
  waiting for transfers between devices: 15.1 us -> 13.7 us
    ppermute x10, waiting for transfers between devices: 12.5 us -> 11.2 us  [swap_apart(): return lax.ppermute(value, ('sx', 'sy'), route)]
    ppermute x10, starting transfers between devices: 9.49 us -> 10.4 us  [swap_apart(): return lax.ppermute(value, ('sx', 'sy'), route)]
  transfers between devices with their start and end apart: 20 -> 20, of which waited for: 10 -> 11; matrix products, arithmetic and copies ran while one was open for 0% -> 0% of each run, Pallas kernels for 17% -> 17%
where the time goes in v3:
time: 66.5 us; the launch traced here: 66.3 us
  starting transfers between devices  35.6 us (54%)
  Pallas kernels  15.8 us (24%)
  waiting for transfers between devices  13.7 us (21%)
  between operations  0.99 us (1%)
    ppermute x4, starting transfers between devices, swap_odd(): return lax.ppermute(block, axis, route + [(b, a) for a, b in route])  15.5 us
    ppermute x10, waiting for transfers between devices, swap_apart(): return lax.ppermute(value, ('sx', 'sy'), route)  11.2 us
    ppermute x10, starting transfers between devices, swap_apart(): return lax.ppermute(value, ('sx', 'sy'), route)  10.4 us
    ppermute x6, starting transfers between devices, swap(): lax.ppermute(block, axis, [(i, i ^ step) for i in range(lax.axis_size(axi...  9.74 us
    pallas_call x1, Pallas kernels, body(): call(last_kernel, shaped(96, TAIL), [VMEM] * 3 + [HBM], [pltpu.VMEM((256,...  3.23 us
    pallas_call x1, Pallas kernels, body(): call(tail_kernel, (shaped(96, 320), placed, placed, turned, turned, wide,...  2.25 us
    pallas_call x1, Pallas kernels, body(): call(side_kernel, (msg, msg, shaped(512, own, dtype=BF16), shaped(512, 51...  1.98 us
    ppermute x6, waiting for transfers between devices, swap(): lax.ppermute(block, axis, [(i, i ^ step) for i in range(lax.axis_size(axi...  1.87 us
  transfers between devices with their start and end apart: 20, of which 11 were waited for; matrix products, arithmetic and copies ran while one was open for 0% of the time, Pallas kernels for 17%

profile of v3, /device:TPU:1, one launch (start us, length us, event | category | flops | bytes accessed | tf_op | source)
XLA Modules:
  0.0 66.3 jit_solution(18237704254020670130)
XLA Ops:
  0.7 0.1 add.71.odd
  0.7 1.8 %gather.1 = (f32[96,128]{1,0:T(8,128)S(1)}, f32[96,128]{1,0:T(8,128)S(1)}, f32[96,128]{1,0:T(8,128)S(1)}, f32[96,128]{1,0:T(8,128)S(1)}, bf16[192,1296]{1,0:T(8,...) custom-call(s32[8,128]{1,0:T(8,128)S(1)} %add.71.odd, s32[1,1,8]{2,1,0:T(1,128)} %count_hbm.1, ...), custom_call_target="tpu_custom_call" | custom-call | flops 254803968 | bytes 2000000 | tf_op jit(solution)/shard_map/gather/pallas_call | solution.py:332
  2.6 2.8 %collective-permute-start = (f32[96,128]{1,0:T(8,128)S(1)}, f32[96,128]{1,0:T(8,128)S(1)}, u32[]{:S(2)}, u32[]{:S(2)}) collective-permute-start(f32[96,128]{1,0:T(8,128)S(1)} %get-tuple-element.51), channel_id=1, source_target_pairs={{32,64},{96,128},{160,192},{224,0},{64,32},{128,96},{192,160},{0,2... | collective-permute-start | bytes 147464 | tf_op jit(solution)/shard_map/ppermute | solution.py:321
  5.3 1.3 %collective-permute-start.1 = (f32[96,128]{1,0:T(8,128)S(1)}, f32[96,128]{1,0:T(8,128)S(1)}, u32[]{:S(2)}, u32[]{:S(2)}) collective-permute-start(f32[96,128]{1,0:T(8,128)S(1)} %get-tuple-element.52), channel_id=1, source_target_pairs={{0,32},{32,0},{64,96},{96,64},{128,160},{160,128},{192,224},{224,1... | collective-permute-start | bytes 147464 | tf_op jit(solution)/shard_map/ppermute | solution.py:315
  6.6 2.3 %tail.1 = (f32[96,320]{1,0:T(8,128)S(1)}, bf16[320,512]{1,0:T(8,128)(2,1)S(1)}, bf16[320,512]{1,0:T(8,128)(2,1)S(1)}, bf16[512,320]{1,0:T(8,128)(2,1)S(1)}, bf16...) custom-call(bf16[192,1296]{1,0:T(8,128)(2,1)S(1)} %get-tuple-element, ...), custom_call_target="tpu_custom_call" | custom-call | flops 238878720 | bytes 6000000 | tf_op jit(solution)/shard_map/tail/pallas_call | solution.py:359
  8.9 0.0 collective-permute-done.sxb
  8.9 0.0 collective-permute-done.1.sxa
  8.9 7.9 %collective-permute-start.3 = (f32[96,128]{1,0:T(8,128)S(1)}, f32[96,128]{1,0:T(8,128)S(1)}, u32[]{:S(2)}, u32[]{:S(2)}) collective-permute-start(f32[96,128]{1,0:T(8,128)S(1)} %get-tuple-element.102), channel_id=1, source_target_pairs={{1,2},{3,4},{5,6},{7,8},{9,10},{11,12},{13,14},{15,16},{17,18},{19... | collective-permute-start | bytes 147464 | tf_op jit(solution)/shard_map/ppermute | solution.py:321
  16.8 0.0 collective-permute-start.2
  16.8 0.9 %head.1 = f32[96,512]{1,0:T(8,128)S(1)} custom-call(bf16[192,1296]{1,0:T(8,128)(2,1)S(1)} %get-tuple-element.53.field, f32[256,256]{1,0:T(8,128)S(1)} %get-tuple-element.60.slab0, f32[256,512]{1,0:T(8,128)S(1)} %get-tuple-element.61.slab1), custom_call_target="tpu_custom_call" | custom-call | flops 226492416 | bytes 1200000 | tf_op jit(solution)/shard_map/head/pallas_call | solution.py:395
  17.7 2.0 %side.1 = (f32[96,128]{1,0:T(8,128)S(1)}, f32[96,128]{1,0:T(8,128)S(1)}, bf16[512,1296]{1,0:T(8,128)(2,1)S(1)}, bf16[512,512]{1,0:T(8,128)(2,1)S(1)}, bf16[256,1...) custom-call(s32[8,128]{1,0:T(8,128)S(1)} %add.71.odd, ...), custom_call_target="tpu_custom_call" | custom-call | flops 382205952 | bytes 3000000 | tf_op jit(solution)/shard_map/side/pallas_call | solution.py:375
  19.7 0.0 collective-permute-done.3.syb
  19.7 0.0 collective-permute-done.2.sya
  19.8 0.6 halo.1
  20.4 1.5 %collective-permute-start.4 = (f32[192,128]{1,0:T(8,128)S(1)}, f32[192,128]{1,0:T(8,128)S(1)}, u32[]{:S(2)}, u32[]{:S(2)}) collective-permute-start(f32[192,128]{1,0:T(8,128)S(1)} %get-tuple-element.74), channel_id=1, source_target_pairs={{0,1},{1,0},{2,3},{3,2},{4,5},{5,4},{6,7},{7,6},{8,9},{9,8},{10,11... | collective-permute-start | bytes 294920 | tf_op jit(solution)/shard_map/ppermute | solution.py:315
  21.9 2.4 %collective-permute-start.5 = (f32[96,128]{1,0:T(8,128)S(1)}, f32[96,128]{1,0:T(8,128)S(1)}, u32[]{:S(2)}, u32[]{:S(2)}) collective-permute-start(f32[96,128]{1,0:T(8,128)S(1)} %get-tuple-element.75), channel_id=1, source_target_pairs={{1,2},{3,4},{5,6},{7,8},{9,10},{11,12},{13,14},{15,16},{17,18},{19... | collective-permute-start | bytes 147464 | tf_op jit(solution)/shard_map/ppermute | solution.py:321
  24.3 3.2 %last.1.own_part = f32[96,1280]{1,0:T(8,128)S(1)} custom-call(bf16[192,1296]{1,0:T(8,128)(2,1)S(1)} %get-tuple-element.53.field, f32[256,1024]{1,0:T(8,128)S(1)} %get-tuple-element.76.slab3, f32[96,512]{1,0:T(8,128)S(1)} %head.1, f32[1,1,1600,1600]{3,2,1,0:T(8,128)} %factor.7), custom_call_target="tpu_custom_call" | custom-call | flops 905969664 | bytes 3000000 | tf_op jit(solution)/shard_map/last/pallas_call | solution.py:416
  27.5 0.7 collective-permute-done.5.ryb
  28.2 0.0 collective-permute-done.4.rya
  28.2 2.5 %collective-permute-start.7 = (f32[96,128]{1,0:T(8,128)S(1)}, f32[96,128]{1,0:T(8,128)S(1)}, u32[]{:S(2)}, u32[]{:S(2)}) collective-permute-start(f32[96,128]{1,0:T(8,128)S(1)} %get-tuple-element.100), channel_id=1, source_target_pairs={{32,64},{96,128},{160,192},{224,0},{64,32},{128,96},{192,160},{0,2... | collective-permute-start | bytes 147464 | tf_op jit(solution)/shard_map/ppermute | solution.py:321
  30.7 0.0 collective-permute-start.6
  30.7 1.8 %local.1 = (f32[96,1296]{1,0:T(8,128)S(1)}, f32[96,512]{1,0:T(8,128)S(1)}, f32[288,96]{1,0:T(8,128)S(1)}) custom-call(f32[96,1280]{1,0:T(8,128)S(1)} %last.1.own_part, f32[96,320]{1,0:T(8,128)S(1)} %get-tuple-element.83.half, bf16[320,1296]{1,0:T(8,128)(2,1)S(1)} %get-tuple-element.84.oh, bf16[320,1296]{1,0:T(8,128)(2,1)S(1)} %get-tuple-element.85.olo, ...), custom_call_target="tpu_custom_call" | custom-call | flops 821145600 | bytes 4000000 | tf_op jit(solution)/shard_map/local/pallas_call | solution.py:430
  32.5 0.0 collective-permute-done.7.rxb
  32.5 0.0 collective-permute-done.6.rxa
  32.5 0.8 %gram.1 = (f32[144,128]{1,0:T(8,128)S(1)}, f32[144,128]{1,0:T(8,128)S(1)}, f32[96,512]{1,0:T(8,128)S(1)}) custom-call(s32[8,128]{1,0:T(8,128)S(1)} %add.71.odd, f32[96,128]{1,0:T(8,128)S(1)} %collective-permute-done.6.rxa, f32[96,128]{1,0:T(8,128)S(1)} %collective-permute-done.7.rxb, f32[192,128]{1,0:T(8,128)S(1)} %collective-permute-done.4.rya, ...), custom_call_target="tpu_custom_call" | custom-call | flops 265420800 | bytes 2000000 | tf_op jit(solution)/shard_map/gram/pallas_call | solution.py:439
  33.3 2.6 %collective-permute-start.8 = (f32[144,128]{1,0:T(8,128)S(1)}, f32[144,128]{1,0:T(8,128)S(1)}, u32[]{:S(2)}, u32[]{:S(2)}) collective-permute-start(f32[144,128]{1,0:T(8,128)S(1)} %get-tuple-element.95), channel_id=1, source_target_pairs={{0,32},{32,0},{64,96},{96,64},{128,160},{160,128},{192,224},{224,1... | collective-permute-start | bytes 221192 | tf_op jit(solution)/shard_map/ppermute | solution.py:315
  35.9 0.9 %collective-permute-done.8 = f32[144,128]{1,0:T(8,128)S(1)} collective-permute-done((f32[144,128]{1,0:T(8,128)S(1)}, f32[144,128]{1,0:T(8,128)S(1)}, u32[]{:S(2)}, u32[]{:S(2)}) %collective-permute-start.8) | collective-permute-done | bytes 73760 | tf_op jit(solution)/shard_map/ppermute | solution.py:315
  36.8 0.1 collective-permute-start.11
  36.9 0.2 collective-permute-start.10
  37.1 2.5 %collective-permute-start.9 = (f32[144,128]{1,0:T(8,128)S(1)}, f32[144,128]{1,0:T(8,128)S(1)}, u32[]{:S(2)}, u32[]{:S(2)}) collective-permute-start(f32[144,128]{1,0:T(8,128)S(1)} %add.78), channel_id=1, source_target_pairs={{0,64},{1,65},{2,66},{3,67},{4,68},{5,69},{6,70},{7,71},{8,72},{9,... | collective-permute-start | bytes 221192 | tf_op jit(solution)/shard_map/ppermute | solution.py:465
  39.5 2.2 %collective-permute-done.11 = f32[144,128]{1,0:T(8,128)S(1)} collective-permute-done((f32[144,128]{1,0:T(8,128)S(1)}, f32[144,128]{1,0:T(8,128)S(1)}, u32[]{:S(2)}, u32[]{:S(2)}) %collective-permute-start.11) | collective-permute-done | bytes 73760 | tf_op jit(solution)/shard_map/ppermute | solution.py:465
  41.7 0.8 %collective-permute-done.10 = f32[144,128]{1,0:T(8,128)S(1)} collective-permute-done((f32[144,128]{1,0:T(8,128)S(1)}, f32[144,128]{1,0:T(8,128)S(1)}, u32[]{:S(2)}, u32[]{:S(2)}) %collective-permute-start.10) | collective-permute-done | bytes 73760 | tf_op jit(solution)/shard_map/ppermute | solution.py:465
  42.5 0.0 collective-permute-done.9
  42.5 0.6 collective-permute-start.14
  43.1 1.1 %collective-permute-start.13 = (f32[144,128]{1,0:T(8,128)S(1)}, f32[144,128]{1,0:T(8,128)S(1)}, u32[]{:S(2)}, u32[]{:S(2)}) collective-permute-start(f32[144,128]{1,0:T(8,128)S(1)} %add_add_fusion.1), channel_id=1, source_target_pairs={{0,24},{1,25},{2,26},{3,27},{4,28},{5,29},{6,30},{7,31},{8,16},{9,... | collective-permute-start | bytes 221192 | tf_op jit(solution)/shard_map/ppermute | solution.py:465
  44.2 1.1 %collective-permute-start.12 = (f32[144,128]{1,0:T(8,128)S(1)}, f32[144,128]{1,0:T(8,128)S(1)}, u32[]{:S(2)}, u32[]{:S(2)}) collective-permute-start(f32[144,128]{1,0:T(8,128)S(1)} %add_add_fusion.1), channel_id=1, source_target_pairs={{0,8},{1,9},{2,10},{3,11},{4,12},{5,13},{6,14},{7,15},{8,0},{9,1},... | collective-permute-start | bytes 221192 | tf_op jit(solution)/shard_map/ppermute | solution.py:465
  45.2 2.1 %collective-permute-done.14 = f32[144,128]{1,0:T(8,128)S(1)} collective-permute-done((f32[144,128]{1,0:T(8,128)S(1)}, f32[144,128]{1,0:T(8,128)S(1)}, u32[]{:S(2)}, u32[]{:S(2)}) %collective-permute-start.14) | collective-permute-done | bytes 73760 | tf_op jit(solution)/shard_map/ppermute | solution.py:465
  47.4 0.7 %collective-permute-done.13 = f32[144,128]{1,0:T(8,128)S(1)} collective-permute-done((f32[144,128]{1,0:T(8,128)S(1)}, f32[144,128]{1,0:T(8,128)S(1)}, u32[]{:S(2)}, u32[]{:S(2)}) %collective-permute-start.13) | collective-permute-done | bytes 73760 | tf_op jit(solution)/shard_map/ppermute | solution.py:465
  48.1 0.0 collective-permute-done.12
  48.1 0.1 collective-permute-start.15
  48.2 1.3 %update.1 = f32[96,1296]{1,0:T(8,128)} custom-call(f32[96,512]{1,0:T(8,128)S(1)} %get-tuple-element.96.back, bf16[512,1296]{1,0:T(8,128)(2,1)S(1)} %get-tuple-element.86.turned, f32[96,1296]{1,0:T(8,128)S(1)} %get-tuple-element.97.local), custom_call_target="tpu_custom_call" | custom-call | flops 254803968 | bytes 3000000 | tf_op jit(solution)/shard_map/update/pallas_call | solution.py:448
  49.5 2.8 %collective-permute-done.15 = f32[144,128]{1,0:T(8,128)S(1)} collective-permute-done((f32[144,128]{1,0:T(8,128)S(1)}, f32[144,128]{1,0:T(8,128)S(1)}, u32[]{:S(2)}, u32[]{:S(2)}) %collective-permute-start.15) | collective-permute-done | bytes 73760 | tf_op jit(solution)/shard_map/ppermute | solution.py:465
  52.3 0.1 collective-permute-start.17
  52.4 0.4 collective-permute-start.18
  52.8 4.4 %collective-permute-start.16 = (f32[144,128]{1,0:T(8,128)S(1)}, f32[144,128]{1,0:T(8,128)S(1)}, u32[]{:S(2)}, u32[]{:S(2)}) collective-permute-start(f32[144,128]{1,0:T(8,128)S(1)} %add.85), channel_id=1, source_target_pairs={{0,1},{1,0},{2,3},{3,2},{4,5},{5,4},{6,7},{7,6},{8,9},{9,8},{10,11... | collective-permute-start | bytes 221192 | tf_op jit(solution)/shard_map/ppermute | solution.py:465
  57.2 0.6 collective-permute-done.17
  57.8 0.1 collective-permute-done.18
  57.9 1.8 %collective-permute-done.16 = f32[144,128]{1,0:T(8,128)S(1)} collective-permute-done((f32[144,128]{1,0:T(8,128)S(1)}, f32[144,128]{1,0:T(8,128)S(1)}, u32[]{:S(2)}, u32[]{:S(2)}) %collective-permute-start.16) | collective-permute-done | bytes 73760 | tf_op jit(solution)/shard_map/ppermute | solution.py:465
  59.8 4.3 %collective-permute-start.19 = (f32[192,128]{1,0:T(8,128)S(1)}, f32[192,128]{1,0:T(8,128)S(1)}, u32[]{:S(2)}, u32[]{:S(2)}) collective-permute-start(f32[192,128]{1,0:T(8,128)S(1)} %pad_maximum_fusion.refs_0_), channel_id=1, source_target_pairs={{0,32},{32,0},{64,96},{96,64},{128,160},{160,128},{192,224},{224,1... | collective-permute-start | bytes 294920 | tf_op jit(solution)/shard_map/ppermute | solution.py:315
  64.1 0.9 %collective-permute-done.19.refs_1_ = f32[192,128]{1,0:T(8,128)S(1)} collective-permute-done((f32[192,128]{1,0:T(8,128)S(1)}, f32[192,128]{1,0:T(8,128)S(1)}, u32[]{:S(2)}, u32[]{:S(2)}) %collective-permute-start.19) | collective-permute-done | bytes 98336 | tf_op jit(solution)/shard_map/ppermute | solution.py:315
  65.1 1.1 %final.1 = f32[288,288]{1,0:T(8,128)} custom-call(s32[8,128]{1,0:T(8,128)S(1)} %add.71.odd, f32[192,128]{1,0:T(8,128)S(1)} %pad_maximum_fusion.refs_0_, f32[192,128]{1,0:T(8,128)S(1)} %collective-permute-done.19.refs_1_), custom_call_target="tpu_custom_call" | custom-call | flops 1000000 | bytes 700000 | tf_op jit(solution)/shard_map/final/pallas_call | solution.py:492
  (12 shorter events, 0.1 us)
Async XLA Ops:
  2.6 6.3 %collective-permute-start = (f32[96,128]{1,0:T(8,128)S(1)}, f32[96,128]{1,0:T(8,128)S(1)}, u32[]{:S(2)}, u32[]{:S(2)}) collective-permute-start(f32[96,128]{1,0:T(8,128)S(1)} %get-tuple-element.51), channel_id=1, source_target_pairs={{32,64},{96,128},{160,192},{224,0},{64,32},{128,96},{192,160},{0,2... | collective-permute-start | bytes 147464 | tf_op jit(solution)/shard_map/ppermute | solution.py:321
  5.3 3.6 %collective-permute-start.1 = (f32[96,128]{1,0:T(8,128)S(1)}, f32[96,128]{1,0:T(8,128)S(1)}, u32[]{:S(2)}, u32[]{:S(2)}) collective-permute-start(f32[96,128]{1,0:T(8,128)S(1)} %get-tuple-element.52), channel_id=1, source_target_pairs={{0,32},{32,0},{64,96},{96,64},{128,160},{160,128},{192,224},{224,1... | collective-permute-start | bytes 147464 | tf_op jit(solution)/shard_map/ppermute | solution.py:315
  8.9 10.8 %collective-permute-start.3 = (f32[96,128]{1,0:T(8,128)S(1)}, f32[96,128]{1,0:T(8,128)S(1)}, u32[]{:S(2)}, u32[]{:S(2)}) collective-permute-start(f32[96,128]{1,0:T(8,128)S(1)} %get-tuple-element.102), channel_id=1, source_target_pairs={{1,2},{3,4},{5,6},{7,8},{9,10},{11,12},{13,14},{15,16},{17,18},{19... | collective-permute-start | bytes 147464 | tf_op jit(solution)/shard_map/ppermute | solution.py:321
  16.8 3.0 %collective-permute-start.2 = (f32[96,128]{1,0:T(8,128)S(1)}, f32[96,128]{1,0:T(8,128)S(1)}, u32[]{:S(2)}, u32[]{:S(2)}) collective-permute-start(f32[96,128]{1,0:T(8,128)S(1)} %get-tuple-element.103), channel_id=1, source_target_pairs={{0,1},{1,0},{2,3},{3,2},{4,5},{5,4},{6,7},{7,6},{8,9},{9,8},{10,11... | collective-permute-start | bytes 147464 | tf_op jit(solution)/shard_map/ppermute | solution.py:315
  20.4 7.8 %collective-permute-start.4 = (f32[192,128]{1,0:T(8,128)S(1)}, f32[192,128]{1,0:T(8,128)S(1)}, u32[]{:S(2)}, u32[]{:S(2)}) collective-permute-start(f32[192,128]{1,0:T(8,128)S(1)} %get-tuple-element.74), channel_id=1, source_target_pairs={{0,1},{1,0},{2,3},{3,2},{4,5},{5,4},{6,7},{7,6},{8,9},{9,8},{10,11... | collective-permute-start | bytes 294920 | tf_op jit(solution)/shard_map/ppermute | solution.py:315
  21.9 6.3 %collective-permute-start.5 = (f32[96,128]{1,0:T(8,128)S(1)}, f32[96,128]{1,0:T(8,128)S(1)}, u32[]{:S(2)}, u32[]{:S(2)}) collective-permute-start(f32[96,128]{1,0:T(8,128)S(1)} %get-tuple-element.75), channel_id=1, source_target_pairs={{1,2},{3,4},{5,6},{7,8},{9,10},{11,12},{13,14},{15,16},{17,18},{19... | collective-permute-start | bytes 147464 | tf_op jit(solution)/shard_map/ppermute | solution.py:321
  28.2 4.3 %collective-permute-start.7 = (f32[96,128]{1,0:T(8,128)S(1)}, f32[96,128]{1,0:T(8,128)S(1)}, u32[]{:S(2)}, u32[]{:S(2)}) collective-permute-start(f32[96,128]{1,0:T(8,128)S(1)} %get-tuple-element.100), channel_id=1, source_target_pairs={{32,64},{96,128},{160,192},{224,0},{64,32},{128,96},{192,160},{0,2... | collective-permute-start | bytes 147464 | tf_op jit(solution)/shard_map/ppermute | solution.py:321
  30.7 1.8 %collective-permute-start.6 = (f32[96,128]{1,0:T(8,128)S(1)}, f32[96,128]{1,0:T(8,128)S(1)}, u32[]{:S(2)}, u32[]{:S(2)}) collective-permute-start(f32[96,128]{1,0:T(8,128)S(1)} %get-tuple-element.101), channel_id=1, source_target_pairs={{0,32},{32,0},{64,96},{96,64},{128,160},{160,128},{192,224},{224,1... | collective-permute-start | bytes 147464 | tf_op jit(solution)/shard_map/ppermute | solution.py:315
  33.3 3.5 %collective-permute-start.8 = (f32[144,128]{1,0:T(8,128)S(1)}, f32[144,128]{1,0:T(8,128)S(1)}, u32[]{:S(2)}, u32[]{:S(2)}) collective-permute-start(f32[144,128]{1,0:T(8,128)S(1)} %get-tuple-element.95), channel_id=1, source_target_pairs={{0,32},{32,0},{64,96},{96,64},{128,160},{160,128},{192,224},{224,1... | collective-permute-start | bytes 221192 | tf_op jit(solution)/shard_map/ppermute | solution.py:315
  36.8 4.9 %collective-permute-start.11 = (f32[144,128]{1,0:T(8,128)S(1)}, f32[144,128]{1,0:T(8,128)S(1)}, u32[]{:S(2)}, u32[]{:S(2)}) collective-permute-start(f32[144,128]{1,0:T(8,128)S(1)} %add.78), channel_id=1, source_target_pairs={{0,128},{1,129},{2,130},{3,131},{4,132},{5,133},{6,134},{7,135},{8... | collective-permute-start | bytes 221192 | tf_op jit(solution)/shard_map/ppermute | solution.py:465
  36.9 5.6 %collective-permute-start.10 = (f32[144,128]{1,0:T(8,128)S(1)}, f32[144,128]{1,0:T(8,128)S(1)}, u32[]{:S(2)}, u32[]{:S(2)}) collective-permute-start(f32[144,128]{1,0:T(8,128)S(1)} %add.78), channel_id=1, source_target_pairs={{0,192},{1,193},{2,194},{3,195},{4,196},{5,197},{6,198},{7,199},{8... | collective-permute-start | bytes 221192 | tf_op jit(solution)/shard_map/ppermute | solution.py:465
  37.1 5.4 %collective-permute-start.9 = (f32[144,128]{1,0:T(8,128)S(1)}, f32[144,128]{1,0:T(8,128)S(1)}, u32[]{:S(2)}, u32[]{:S(2)}) collective-permute-start(f32[144,128]{1,0:T(8,128)S(1)} %add.78), channel_id=1, source_target_pairs={{0,64},{1,65},{2,66},{3,67},{4,68},{5,69},{6,70},{7,71},{8,72},{9,... | collective-permute-start | bytes 221192 | tf_op jit(solution)/shard_map/ppermute | solution.py:465
  42.5 4.9 %collective-permute-start.14 = (f32[144,128]{1,0:T(8,128)S(1)}, f32[144,128]{1,0:T(8,128)S(1)}, u32[]{:S(2)}, u32[]{:S(2)}) collective-permute-start(f32[144,128]{1,0:T(8,128)S(1)} %add_add_fusion.1), channel_id=1, source_target_pairs={{0,16},{1,17},{2,18},{3,19},{4,20},{5,21},{6,22},{7,23},{8,24},{9,... | collective-permute-start | bytes 221192 | tf_op jit(solution)/shard_map/ppermute | solution.py:465
  43.1 5.0 %collective-permute-start.13 = (f32[144,128]{1,0:T(8,128)S(1)}, f32[144,128]{1,0:T(8,128)S(1)}, u32[]{:S(2)}, u32[]{:S(2)}) collective-permute-start(f32[144,128]{1,0:T(8,128)S(1)} %add_add_fusion.1), channel_id=1, source_target_pairs={{0,24},{1,25},{2,26},{3,27},{4,28},{5,29},{6,30},{7,31},{8,16},{9,... | collective-permute-start | bytes 221192 | tf_op jit(solution)/shard_map/ppermute | solution.py:465
  44.2 3.9 %collective-permute-start.12 = (f32[144,128]{1,0:T(8,128)S(1)}, f32[144,128]{1,0:T(8,128)S(1)}, u32[]{:S(2)}, u32[]{:S(2)}) collective-permute-start(f32[144,128]{1,0:T(8,128)S(1)} %add_add_fusion.1), channel_id=1, source_target_pairs={{0,8},{1,9},{2,10},{3,11},{4,12},{5,13},{6,14},{7,15},{8,0},{9,1},... | collective-permute-start | bytes 221192 | tf_op jit(solution)/shard_map/ppermute | solution.py:465
  48.1 4.2 %collective-permute-start.15 = (f32[144,128]{1,0:T(8,128)S(1)}, f32[144,128]{1,0:T(8,128)S(1)}, u32[]{:S(2)}, u32[]{:S(2)}) collective-permute-start(f32[144,128]{1,0:T(8,128)S(1)} %add_add_fusion), channel_id=1, source_target_pairs={{0,6},{1,7},{2,4},{3,5},{4,2},{5,3},{6,0},{7,1},{8,14},{9,15},{10,... | collective-permute-start | bytes 221192 | tf_op jit(solution)/shard_map/ppermute | solution.py:465
  52.3 5.5 %collective-permute-start.17 = (f32[144,128]{1,0:T(8,128)S(1)}, f32[144,128]{1,0:T(8,128)S(1)}, u32[]{:S(2)}, u32[]{:S(2)}) collective-permute-start(f32[144,128]{1,0:T(8,128)S(1)} %add.85), channel_id=1, source_target_pairs={{0,2},{1,3},{2,0},{3,1},{4,6},{5,7},{6,4},{7,5},{8,10},{9,11},{10,... | collective-permute-start | bytes 221192 | tf_op jit(solution)/shard_map/ppermute | solution.py:465
  52.4 5.5 %collective-permute-start.18 = (f32[144,128]{1,0:T(8,128)S(1)}, f32[144,128]{1,0:T(8,128)S(1)}, u32[]{:S(2)}, u32[]{:S(2)}) collective-permute-start(f32[144,128]{1,0:T(8,128)S(1)} %add.85), channel_id=1, source_target_pairs={{0,3},{1,2},{2,1},{3,0},{4,7},{5,6},{6,5},{7,4},{8,11},{9,10},{10,... | collective-permute-start | bytes 221192 | tf_op jit(solution)/shard_map/ppermute | solution.py:465
  52.8 7.0 %collective-permute-start.16 = (f32[144,128]{1,0:T(8,128)S(1)}, f32[144,128]{1,0:T(8,128)S(1)}, u32[]{:S(2)}, u32[]{:S(2)}) collective-permute-start(f32[144,128]{1,0:T(8,128)S(1)} %add.85), channel_id=1, source_target_pairs={{0,1},{1,0},{2,3},{3,2},{4,5},{5,4},{6,7},{7,6},{8,9},{9,8},{10,11... | collective-permute-start | bytes 221192 | tf_op jit(solution)/shard_map/ppermute | solution.py:465
  59.8 5.3 %collective-permute-start.19 = (f32[192,128]{1,0:T(8,128)S(1)}, f32[192,128]{1,0:T(8,128)S(1)}, u32[]{:S(2)}, u32[]{:S(2)}) collective-permute-start(f32[192,128]{1,0:T(8,128)S(1)} %pad_maximum_fusion.refs_0_), channel_id=1, source_target_pairs={{0,32},{32,0},{64,96},{96,64},{128,160},{160,128},{192,224},{224,1... | collective-permute-start | bytes 294920 | tf_op jit(solution)/shard_map/ppermute | solution.py:315

commit v4 on v3

--- a/solution.py
+++ b/solution.py
@@ -422,7 +422,7 @@
         moved=3000000,
         name="last",
     )(field, slab3, head, factor)
-    rya, ryb, own_part = lax.optimization_barrier((rya, ryb, own_part))
+    ryb, rya, own_part = lax.optimization_barrier((ryb, rya, own_part))
 
     relay = jnp.where(lane >= EDGE, rya[:96] + ryb, 0.0)
     rxb, rxa = swap_odd(bxb + relay, "sx"), swap(bxa + relay, "sx", 1)

time: 66.5 us -> 66.5 us (level)
  no operation moved by 1% of the time
where the time goes in v4:
time: 66.5 us; the launch traced here: 66.3 us
  starting transfers between devices  35.6 us (54%)
  Pallas kernels  15.8 us (24%)
  waiting for transfers between devices  13.7 us (21%)
  between operations  0.99 us (1%)
    ppermute x4, starting transfers between devices, swap_odd(): return lax.ppermute(block, axis, route + [(b, a) for a, b in route])  15.5 us
    ppermute x10, waiting for transfers between devices, swap_apart(): return lax.ppermute(value, ('sx', 'sy'), route)  11.2 us
    ppermute x10, starting transfers between devices, swap_apart(): return lax.ppermute(value, ('sx', 'sy'), route)  10.4 us
    ppermute x6, starting transfers between devices, swap(): lax.ppermute(block, axis, [(i, i ^ step) for i in range(lax.axis_size(axi...  9.74 us
    pallas_call x1, Pallas kernels, body(): call(last_kernel, shaped(96, TAIL), [VMEM] * 3 + [HBM], [pltpu.VMEM((256,...  3.23 us
    pallas_call x1, Pallas kernels, body(): call(tail_kernel, (shaped(96, 320), placed, placed, turned, turned, wide,...  2.25 us
    pallas_call x1, Pallas kernels, body(): call(side_kernel, (msg, msg, shaped(512, own, dtype=BF16), shaped(512, 51...  1.98 us
    ppermute x6, waiting for transfers between devices, swap(): lax.ppermute(block, axis, [(i, i ^ step) for i in range(lax.axis_size(axi...  1.87 us
  transfers between devices with their start and end apart: 20, of which 11 were waited for; matrix products, arithmetic and copies ran while one was open for 0% of the time, Pallas kernels for 17%

profile of v4, /device:TPU:1, one launch (start us, length us, event | category | flops | bytes accessed | tf_op | source)
XLA Modules:
  0.0 66.3 jit_solution(18237704254020670130)
XLA Ops:
  0.7 0.1 add.71.odd
  0.7 1.8 %gather.1 = (f32[96,128]{1,0:T(8,128)S(1)}, f32[96,128]{1,0:T(8,128)S(1)}, f32[96,128]{1,0:T(8,128)S(1)}, f32[96,128]{1,0:T(8,128)S(1)}, bf16[192,1296]{1,0:T(8,...) custom-call(s32[8,128]{1,0:T(8,128)S(1)} %add.71.odd, s32[1,1,8]{2,1,0:T(1,128)} %count_hbm.1, ...), custom_call_target="tpu_custom_call" | custom-call | flops 254803968 | bytes 2000000 | tf_op jit(solution)/shard_map/gather/pallas_call | solution.py:332
  2.6 2.8 %collective-permute-start = (f32[96,128]{1,0:T(8,128)S(1)}, f32[96,128]{1,0:T(8,128)S(1)}, u32[]{:S(2)}, u32[]{:S(2)}) collective-permute-start(f32[96,128]{1,0:T(8,128)S(1)} %get-tuple-element.51), channel_id=1, source_target_pairs={{32,64},{96,128},{160,192},{224,0},{64,32},{128,96},{192,160},{0,2... | collective-permute-start | bytes 147464 | tf_op jit(solution)/shard_map/ppermute | solution.py:321
  5.3 1.3 %collective-permute-start.1 = (f32[96,128]{1,0:T(8,128)S(1)}, f32[96,128]{1,0:T(8,128)S(1)}, u32[]{:S(2)}, u32[]{:S(2)}) collective-permute-start(f32[96,128]{1,0:T(8,128)S(1)} %get-tuple-element.52), channel_id=1, source_target_pairs={{0,32},{32,0},{64,96},{96,64},{128,160},{160,128},{192,224},{224,1... | collective-permute-start | bytes 147464 | tf_op jit(solution)/shard_map/ppermute | solution.py:315
  6.6 2.3 %tail.1 = (f32[96,320]{1,0:T(8,128)S(1)}, bf16[320,512]{1,0:T(8,128)(2,1)S(1)}, bf16[320,512]{1,0:T(8,128)(2,1)S(1)}, bf16[512,320]{1,0:T(8,128)(2,1)S(1)}, bf16...) custom-call(bf16[192,1296]{1,0:T(8,128)(2,1)S(1)} %get-tuple-element, ...), custom_call_target="tpu_custom_call" | custom-call | flops 238878720 | bytes 6000000 | tf_op jit(solution)/shard_map/tail/pallas_call | solution.py:359
  8.9 0.0 collective-permute-done.sxb
  8.9 0.0 collective-permute-done.1.sxa
  8.9 7.9 %collective-permute-start.3 = (f32[96,128]{1,0:T(8,128)S(1)}, f32[96,128]{1,0:T(8,128)S(1)}, u32[]{:S(2)}, u32[]{:S(2)}) collective-permute-start(f32[96,128]{1,0:T(8,128)S(1)} %get-tuple-element.102), channel_id=1, source_target_pairs={{1,2},{3,4},{5,6},{7,8},{9,10},{11,12},{13,14},{15,16},{17,18},{19... | collective-permute-start | bytes 147464 | tf_op jit(solution)/shard_map/ppermute | solution.py:321
  16.8 0.0 collective-permute-start.2
  16.8 0.9 %head.1 = f32[96,512]{1,0:T(8,128)S(1)} custom-call(bf16[192,1296]{1,0:T(8,128)(2,1)S(1)} %get-tuple-element.53.field, f32[256,256]{1,0:T(8,128)S(1)} %get-tuple-element.60.slab0, f32[256,512]{1,0:T(8,128)S(1)} %get-tuple-element.61.slab1), custom_call_target="tpu_custom_call" | custom-call | flops 226492416 | bytes 1200000 | tf_op jit(solution)/shard_map/head/pallas_call | solution.py:395
  17.7 2.0 %side.1 = (f32[96,128]{1,0:T(8,128)S(1)}, f32[96,128]{1,0:T(8,128)S(1)}, bf16[512,1296]{1,0:T(8,128)(2,1)S(1)}, bf16[512,512]{1,0:T(8,128)(2,1)S(1)}, bf16[256,1...) custom-call(s32[8,128]{1,0:T(8,128)S(1)} %add.71.odd, ...), custom_call_target="tpu_custom_call" | custom-call | flops 382205952 | bytes 3000000 | tf_op jit(solution)/shard_map/side/pallas_call | solution.py:375
  19.7 0.0 collective-permute-done.3.syb
  19.7 0.0 collective-permute-done.2.sya
  19.8 0.6 halo.1
  20.4 1.5 %collective-permute-start.5 = (f32[192,128]{1,0:T(8,128)S(1)}, f32[192,128]{1,0:T(8,128)S(1)}, u32[]{:S(2)}, u32[]{:S(2)}) collective-permute-start(f32[192,128]{1,0:T(8,128)S(1)} %get-tuple-element.75), channel_id=1, source_target_pairs={{0,1},{1,0},{2,3},{3,2},{4,5},{5,4},{6,7},{7,6},{8,9},{9,8},{10,11... | collective-permute-start | bytes 294920 | tf_op jit(solution)/shard_map/ppermute | solution.py:315
  21.9 2.4 %collective-permute-start.4 = (f32[96,128]{1,0:T(8,128)S(1)}, f32[96,128]{1,0:T(8,128)S(1)}, u32[]{:S(2)}, u32[]{:S(2)}) collective-permute-start(f32[96,128]{1,0:T(8,128)S(1)} %get-tuple-element.74), channel_id=1, source_target_pairs={{1,2},{3,4},{5,6},{7,8},{9,10},{11,12},{13,14},{15,16},{17,18},{19... | collective-permute-start | bytes 147464 | tf_op jit(solution)/shard_map/ppermute | solution.py:321
  24.3 3.2 %last.1.own_part = f32[96,1280]{1,0:T(8,128)S(1)} custom-call(bf16[192,1296]{1,0:T(8,128)(2,1)S(1)} %get-tuple-element.53.field, f32[256,1024]{1,0:T(8,128)S(1)} %get-tuple-element.76.slab3, f32[96,512]{1,0:T(8,128)S(1)} %head.1, f32[1,1,1600,1600]{3,2,1,0:T(8,128)} %factor.7), custom_call_target="tpu_custom_call" | custom-call | flops 905969664 | bytes 3000000 | tf_op jit(solution)/shard_map/last/pallas_call | solution.py:416
  27.5 0.7 collective-permute-done.4.ryb
  28.2 0.0 collective-permute-done.5.rya
  28.2 2.5 %collective-permute-start.7 = (f32[96,128]{1,0:T(8,128)S(1)}, f32[96,128]{1,0:T(8,128)S(1)}, u32[]{:S(2)}, u32[]{:S(2)}) collective-permute-start(f32[96,128]{1,0:T(8,128)S(1)} %get-tuple-element.100), channel_id=1, source_target_pairs={{32,64},{96,128},{160,192},{224,0},{64,32},{128,96},{192,160},{0,2... | collective-permute-start | bytes 147464 | tf_op jit(solution)/shard_map/ppermute | solution.py:321
  30.7 0.0 collective-permute-start.6
  30.7 1.8 %local.1 = (f32[96,1296]{1,0:T(8,128)S(1)}, f32[96,512]{1,0:T(8,128)S(1)}, f32[288,96]{1,0:T(8,128)S(1)}) custom-call(f32[96,1280]{1,0:T(8,128)S(1)} %last.1.own_part, f32[96,320]{1,0:T(8,128)S(1)} %get-tuple-element.83.half, bf16[320,1296]{1,0:T(8,128)(2,1)S(1)} %get-tuple-element.84.oh, bf16[320,1296]{1,0:T(8,128)(2,1)S(1)} %get-tuple-element.85.olo, ...), custom_call_target="tpu_custom_call" | custom-call | flops 821145600 | bytes 4000000 | tf_op jit(solution)/shard_map/local/pallas_call | solution.py:430
  32.5 0.0 collective-permute-done.7.rxb
  32.5 0.0 collective-permute-done.6.rxa
  32.5 0.8 %gram.1 = (f32[144,128]{1,0:T(8,128)S(1)}, f32[144,128]{1,0:T(8,128)S(1)}, f32[96,512]{1,0:T(8,128)S(1)}) custom-call(s32[8,128]{1,0:T(8,128)S(1)} %add.71.odd, f32[96,128]{1,0:T(8,128)S(1)} %collective-permute-done.6.rxa, f32[96,128]{1,0:T(8,128)S(1)} %collective-permute-done.7.rxb, f32[192,128]{1,0:T(8,128)S(1)} %collective-permute-done.5.rya, ...), custom_call_target="tpu_custom_call" | custom-call | flops 265420800 | bytes 2000000 | tf_op jit(solution)/shard_map/gram/pallas_call | solution.py:439
  33.3 2.6 %collective-permute-start.8 = (f32[144,128]{1,0:T(8,128)S(1)}, f32[144,128]{1,0:T(8,128)S(1)}, u32[]{:S(2)}, u32[]{:S(2)}) collective-permute-start(f32[144,128]{1,0:T(8,128)S(1)} %get-tuple-element.95), channel_id=1, source_target_pairs={{0,32},{32,0},{64,96},{96,64},{128,160},{160,128},{192,224},{224,1... | collective-permute-start | bytes 221192 | tf_op jit(solution)/shard_map/ppermute | solution.py:315
  35.9 0.9 %collective-permute-done.8 = f32[144,128]{1,0:T(8,128)S(1)} collective-permute-done((f32[144,128]{1,0:T(8,128)S(1)}, f32[144,128]{1,0:T(8,128)S(1)}, u32[]{:S(2)}, u32[]{:S(2)}) %collective-permute-start.8) | collective-permute-done | bytes 73760 | tf_op jit(solution)/shard_map/ppermute | solution.py:315
  36.8 0.1 collective-permute-start.11
  36.9 0.2 collective-permute-start.10
  37.1 2.5 %collective-permute-start.9 = (f32[144,128]{1,0:T(8,128)S(1)}, f32[144,128]{1,0:T(8,128)S(1)}, u32[]{:S(2)}, u32[]{:S(2)}) collective-permute-start(f32[144,128]{1,0:T(8,128)S(1)} %add.78), channel_id=1, source_target_pairs={{0,64},{1,65},{2,66},{3,67},{4,68},{5,69},{6,70},{7,71},{8,72},{9,... | collective-permute-start | bytes 221192 | tf_op jit(solution)/shard_map/ppermute | solution.py:465
  39.5 2.2 %collective-permute-done.11 = f32[144,128]{1,0:T(8,128)S(1)} collective-permute-done((f32[144,128]{1,0:T(8,128)S(1)}, f32[144,128]{1,0:T(8,128)S(1)}, u32[]{:S(2)}, u32[]{:S(2)}) %collective-permute-start.11) | collective-permute-done | bytes 73760 | tf_op jit(solution)/shard_map/ppermute | solution.py:465
  41.7 0.8 %collective-permute-done.10 = f32[144,128]{1,0:T(8,128)S(1)} collective-permute-done((f32[144,128]{1,0:T(8,128)S(1)}, f32[144,128]{1,0:T(8,128)S(1)}, u32[]{:S(2)}, u32[]{:S(2)}) %collective-permute-start.10) | collective-permute-done | bytes 73760 | tf_op jit(solution)/shard_map/ppermute | solution.py:465
  42.5 0.0 collective-permute-done.9
  42.5 0.6 collective-permute-start.14
  43.1 1.1 %collective-permute-start.13 = (f32[144,128]{1,0:T(8,128)S(1)}, f32[144,128]{1,0:T(8,128)S(1)}, u32[]{:S(2)}, u32[]{:S(2)}) collective-permute-start(f32[144,128]{1,0:T(8,128)S(1)} %add_add_fusion.1), channel_id=1, source_target_pairs={{0,24},{1,25},{2,26},{3,27},{4,28},{5,29},{6,30},{7,31},{8,16},{9,... | collective-permute-start | bytes 221192 | tf_op jit(solution)/shard_map/ppermute | solution.py:465
  44.2 1.1 %collective-permute-start.12 = (f32[144,128]{1,0:T(8,128)S(1)}, f32[144,128]{1,0:T(8,128)S(1)}, u32[]{:S(2)}, u32[]{:S(2)}) collective-permute-start(f32[144,128]{1,0:T(8,128)S(1)} %add_add_fusion.1), channel_id=1, source_target_pairs={{0,8},{1,9},{2,10},{3,11},{4,12},{5,13},{6,14},{7,15},{8,0},{9,1},... | collective-permute-start | bytes 221192 | tf_op jit(solution)/shard_map/ppermute | solution.py:465
  45.2 2.1 %collective-permute-done.14 = f32[144,128]{1,0:T(8,128)S(1)} collective-permute-done((f32[144,128]{1,0:T(8,128)S(1)}, f32[144,128]{1,0:T(8,128)S(1)}, u32[]{:S(2)}, u32[]{:S(2)}) %collective-permute-start.14) | collective-permute-done | bytes 73760 | tf_op jit(solution)/shard_map/ppermute | solution.py:465
  47.4 0.7 %collective-permute-done.13 = f32[144,128]{1,0:T(8,128)S(1)} collective-permute-done((f32[144,128]{1,0:T(8,128)S(1)}, f32[144,128]{1,0:T(8,128)S(1)}, u32[]{:S(2)}, u32[]{:S(2)}) %collective-permute-start.13) | collective-permute-done | bytes 73760 | tf_op jit(solution)/shard_map/ppermute | solution.py:465
  48.1 0.0 collective-permute-done.12
  48.1 0.1 collective-permute-start.15
  48.2 1.3 %update.1 = f32[96,1296]{1,0:T(8,128)} custom-call(f32[96,512]{1,0:T(8,128)S(1)} %get-tuple-element.96.back, bf16[512,1296]{1,0:T(8,128)(2,1)S(1)} %get-tuple-element.86.turned, f32[96,1296]{1,0:T(8,128)S(1)} %get-tuple-element.97.local), custom_call_target="tpu_custom_call" | custom-call | flops 254803968 | bytes 3000000 | tf_op jit(solution)/shard_map/update/pallas_call | solution.py:448
  49.5 2.8 %collective-permute-done.15 = f32[144,128]{1,0:T(8,128)S(1)} collective-permute-done((f32[144,128]{1,0:T(8,128)S(1)}, f32[144,128]{1,0:T(8,128)S(1)}, u32[]{:S(2)}, u32[]{:S(2)}) %collective-permute-start.15) | collective-permute-done | bytes 73760 | tf_op jit(solution)/shard_map/ppermute | solution.py:465
  52.3 0.1 collective-permute-start.17
  52.4 0.4 collective-permute-start.18
  52.8 4.4 %collective-permute-start.16 = (f32[144,128]{1,0:T(8,128)S(1)}, f32[144,128]{1,0:T(8,128)S(1)}, u32[]{:S(2)}, u32[]{:S(2)}) collective-permute-start(f32[144,128]{1,0:T(8,128)S(1)} %add.85), channel_id=1, source_target_pairs={{0,1},{1,0},{2,3},{3,2},{4,5},{5,4},{6,7},{7,6},{8,9},{9,8},{10,11... | collective-permute-start | bytes 221192 | tf_op jit(solution)/shard_map/ppermute | solution.py:465
  57.2 0.6 collective-permute-done.17
  57.8 0.1 collective-permute-done.18
  57.9 1.8 %collective-permute-done.16 = f32[144,128]{1,0:T(8,128)S(1)} collective-permute-done((f32[144,128]{1,0:T(8,128)S(1)}, f32[144,128]{1,0:T(8,128)S(1)}, u32[]{:S(2)}, u32[]{:S(2)}) %collective-permute-start.16) | collective-permute-done | bytes 73760 | tf_op jit(solution)/shard_map/ppermute | solution.py:465
  59.8 4.3 %collective-permute-start.19 = (f32[192,128]{1,0:T(8,128)S(1)}, f32[192,128]{1,0:T(8,128)S(1)}, u32[]{:S(2)}, u32[]{:S(2)}) collective-permute-start(f32[192,128]{1,0:T(8,128)S(1)} %pad_maximum_fusion.refs_0_), channel_id=1, source_target_pairs={{0,32},{32,0},{64,96},{96,64},{128,160},{160,128},{192,224},{224,1... | collective-permute-start | bytes 294920 | tf_op jit(solution)/shard_map/ppermute | solution.py:315
  64.1 0.9 %collective-permute-done.19.refs_1_ = f32[192,128]{1,0:T(8,128)S(1)} collective-permute-done((f32[192,128]{1,0:T(8,128)S(1)}, f32[192,128]{1,0:T(8,128)S(1)}, u32[]{:S(2)}, u32[]{:S(2)}) %collective-permute-start.19) | collective-permute-done | bytes 98336 | tf_op jit(solution)/shard_map/ppermute | solution.py:315
  65.1 1.1 %final.1 = f32[288,288]{1,0:T(8,128)} custom-call(s32[8,128]{1,0:T(8,128)S(1)} %add.71.odd, f32[192,128]{1,0:T(8,128)S(1)} %pad_maximum_fusion.refs_0_, f32[192,128]{1,0:T(8,128)S(1)} %collective-permute-done.19.refs_1_), custom_call_target="tpu_custom_call" | custom-call | flops 1000000 | bytes 700000 | tf_op jit(solution)/shard_map/final/pallas_call | solution.py:492
  (12 shorter events, 0.1 us)
Async XLA Ops:
  2.6 6.3 %collective-permute-start = (f32[96,128]{1,0:T(8,128)S(1)}, f32[96,128]{1,0:T(8,128)S(1)}, u32[]{:S(2)}, u32[]{:S(2)}) collective-permute-start(f32[96,128]{1,0:T(8,128)S(1)} %get-tuple-element.51), channel_id=1, source_target_pairs={{32,64},{96,128},{160,192},{224,0},{64,32},{128,96},{192,160},{0,2... | collective-permute-start | bytes 147464 | tf_op jit(solution)/shard_map/ppermute | solution.py:321
  5.3 3.6 %collective-permute-start.1 = (f32[96,128]{1,0:T(8,128)S(1)}, f32[96,128]{1,0:T(8,128)S(1)}, u32[]{:S(2)}, u32[]{:S(2)}) collective-permute-start(f32[96,128]{1,0:T(8,128)S(1)} %get-tuple-element.52), channel_id=1, source_target_pairs={{0,32},{32,0},{64,96},{96,64},{128,160},{160,128},{192,224},{224,1... | collective-permute-start | bytes 147464 | tf_op jit(solution)/shard_map/ppermute | solution.py:315
  8.9 10.8 %collective-permute-start.3 = (f32[96,128]{1,0:T(8,128)S(1)}, f32[96,128]{1,0:T(8,128)S(1)}, u32[]{:S(2)}, u32[]{:S(2)}) collective-permute-start(f32[96,128]{1,0:T(8,128)S(1)} %get-tuple-element.102), channel_id=1, source_target_pairs={{1,2},{3,4},{5,6},{7,8},{9,10},{11,12},{13,14},{15,16},{17,18},{19... | collective-permute-start | bytes 147464 | tf_op jit(solution)/shard_map/ppermute | solution.py:321
  16.8 3.0 %collective-permute-start.2 = (f32[96,128]{1,0:T(8,128)S(1)}, f32[96,128]{1,0:T(8,128)S(1)}, u32[]{:S(2)}, u32[]{:S(2)}) collective-permute-start(f32[96,128]{1,0:T(8,128)S(1)} %get-tuple-element.103), channel_id=1, source_target_pairs={{0,1},{1,0},{2,3},{3,2},{4,5},{5,4},{6,7},{7,6},{8,9},{9,8},{10,11... | collective-permute-start | bytes 147464 | tf_op jit(solution)/shard_map/ppermute | solution.py:315
  20.4 7.8 %collective-permute-start.5 = (f32[192,128]{1,0:T(8,128)S(1)}, f32[192,128]{1,0:T(8,128)S(1)}, u32[]{:S(2)}, u32[]{:S(2)}) collective-permute-start(f32[192,128]{1,0:T(8,128)S(1)} %get-tuple-element.75), channel_id=1, source_target_pairs={{0,1},{1,0},{2,3},{3,2},{4,5},{5,4},{6,7},{7,6},{8,9},{9,8},{10,11... | collective-permute-start | bytes 294920 | tf_op jit(solution)/shard_map/ppermute | solution.py:315
  21.9 6.3 %collective-permute-start.4 = (f32[96,128]{1,0:T(8,128)S(1)}, f32[96,128]{1,0:T(8,128)S(1)}, u32[]{:S(2)}, u32[]{:S(2)}) collective-permute-start(f32[96,128]{1,0:T(8,128)S(1)} %get-tuple-element.74), channel_id=1, source_target_pairs={{1,2},{3,4},{5,6},{7,8},{9,10},{11,12},{13,14},{15,16},{17,18},{19... | collective-permute-start | bytes 147464 | tf_op jit(solution)/shard_map/ppermute | solution.py:321
  28.2 4.3 %collective-permute-start.7 = (f32[96,128]{1,0:T(8,128)S(1)}, f32[96,128]{1,0:T(8,128)S(1)}, u32[]{:S(2)}, u32[]{:S(2)}) collective-permute-start(f32[96,128]{1,0:T(8,128)S(1)} %get-tuple-element.100), channel_id=1, source_target_pairs={{32,64},{96,128},{160,192},{224,0},{64,32},{128,96},{192,160},{0,2... | collective-permute-start | bytes 147464 | tf_op jit(solution)/shard_map/ppermute | solution.py:321
  30.7 1.8 %collective-permute-start.6 = (f32[96,128]{1,0:T(8,128)S(1)}, f32[96,128]{1,0:T(8,128)S(1)}, u32[]{:S(2)}, u32[]{:S(2)}) collective-permute-start(f32[96,128]{1,0:T(8,128)S(1)} %get-tuple-element.101), channel_id=1, source_target_pairs={{0,32},{32,0},{64,96},{96,64},{128,160},{160,128},{192,224},{224,1... | collective-permute-start | bytes 147464 | tf_op jit(solution)/shard_map/ppermute | solution.py:315
  33.3 3.5 %collective-permute-start.8 = (f32[144,128]{1,0:T(8,128)S(1)}, f32[144,128]{1,0:T(8,128)S(1)}, u32[]{:S(2)}, u32[]{:S(2)}) collective-permute-start(f32[144,128]{1,0:T(8,128)S(1)} %get-tuple-element.95), channel_id=1, source_target_pairs={{0,32},{32,0},{64,96},{96,64},{128,160},{160,128},{192,224},{224,1... | collective-permute-start | bytes 221192 | tf_op jit(solution)/shard_map/ppermute | solution.py:315
  36.8 4.9 %collective-permute-start.11 = (f32[144,128]{1,0:T(8,128)S(1)}, f32[144,128]{1,0:T(8,128)S(1)}, u32[]{:S(2)}, u32[]{:S(2)}) collective-permute-start(f32[144,128]{1,0:T(8,128)S(1)} %add.78), channel_id=1, source_target_pairs={{0,128},{1,129},{2,130},{3,131},{4,132},{5,133},{6,134},{7,135},{8... | collective-permute-start | bytes 221192 | tf_op jit(solution)/shard_map/ppermute | solution.py:465
  36.9 5.6 %collective-permute-start.10 = (f32[144,128]{1,0:T(8,128)S(1)}, f32[144,128]{1,0:T(8,128)S(1)}, u32[]{:S(2)}, u32[]{:S(2)}) collective-permute-start(f32[144,128]{1,0:T(8,128)S(1)} %add.78), channel_id=1, source_target_pairs={{0,192},{1,193},{2,194},{3,195},{4,196},{5,197},{6,198},{7,199},{8... | collective-permute-start | bytes 221192 | tf_op jit(solution)/shard_map/ppermute | solution.py:465
  37.1 5.4 %collective-permute-start.9 = (f32[144,128]{1,0:T(8,128)S(1)}, f32[144,128]{1,0:T(8,128)S(1)}, u32[]{:S(2)}, u32[]{:S(2)}) collective-permute-start(f32[144,128]{1,0:T(8,128)S(1)} %add.78), channel_id=1, source_target_pairs={{0,64},{1,65},{2,66},{3,67},{4,68},{5,69},{6,70},{7,71},{8,72},{9,... | collective-permute-start | bytes 221192 | tf_op jit(solution)/shard_map/ppermute | solution.py:465
  42.5 4.9 %collective-permute-start.14 = (f32[144,128]{1,0:T(8,128)S(1)}, f32[144,128]{1,0:T(8,128)S(1)}, u32[]{:S(2)}, u32[]{:S(2)}) collective-permute-start(f32[144,128]{1,0:T(8,128)S(1)} %add_add_fusion.1), channel_id=1, source_target_pairs={{0,16},{1,17},{2,18},{3,19},{4,20},{5,21},{6,22},{7,23},{8,24},{9,... | collective-permute-start | bytes 221192 | tf_op jit(solution)/shard_map/ppermute | solution.py:465
  43.1 5.0 %collective-permute-start.13 = (f32[144,128]{1,0:T(8,128)S(1)}, f32[144,128]{1,0:T(8,128)S(1)}, u32[]{:S(2)}, u32[]{:S(2)}) collective-permute-start(f32[144,128]{1,0:T(8,128)S(1)} %add_add_fusion.1), channel_id=1, source_target_pairs={{0,24},{1,25},{2,26},{3,27},{4,28},{5,29},{6,30},{7,31},{8,16},{9,... | collective-permute-start | bytes 221192 | tf_op jit(solution)/shard_map/ppermute | solution.py:465
  44.2 3.9 %collective-permute-start.12 = (f32[144,128]{1,0:T(8,128)S(1)}, f32[144,128]{1,0:T(8,128)S(1)}, u32[]{:S(2)}, u32[]{:S(2)}) collective-permute-start(f32[144,128]{1,0:T(8,128)S(1)} %add_add_fusion.1), channel_id=1, source_target_pairs={{0,8},{1,9},{2,10},{3,11},{4,12},{5,13},{6,14},{7,15},{8,0},{9,1},... | collective-permute-start | bytes 221192 | tf_op jit(solution)/shard_map/ppermute | solution.py:465
  48.1 4.2 %collective-permute-start.15 = (f32[144,128]{1,0:T(8,128)S(1)}, f32[144,128]{1,0:T(8,128)S(1)}, u32[]{:S(2)}, u32[]{:S(2)}) collective-permute-start(f32[144,128]{1,0:T(8,128)S(1)} %add_add_fusion), channel_id=1, source_target_pairs={{0,6},{1,7},{2,4},{3,5},{4,2},{5,3},{6,0},{7,1},{8,14},{9,15},{10,... | collective-permute-start | bytes 221192 | tf_op jit(solution)/shard_map/ppermute | solution.py:465
  52.3 5.5 %collective-permute-start.17 = (f32[144,128]{1,0:T(8,128)S(1)}, f32[144,128]{1,0:T(8,128)S(1)}, u32[]{:S(2)}, u32[]{:S(2)}) collective-permute-start(f32[144,128]{1,0:T(8,128)S(1)} %add.85), channel_id=1, source_target_pairs={{0,2},{1,3},{2,0},{3,1},{4,6},{5,7},{6,4},{7,5},{8,10},{9,11},{10,... | collective-permute-start | bytes 221192 | tf_op jit(solution)/shard_map/ppermute | solution.py:465
  52.4 5.5 %collective-permute-start.18 = (f32[144,128]{1,0:T(8,128)S(1)}, f32[144,128]{1,0:T(8,128)S(1)}, u32[]{:S(2)}, u32[]{:S(2)}) collective-permute-start(f32[144,128]{1,0:T(8,128)S(1)} %add.85), channel_id=1, source_target_pairs={{0,3},{1,2},{2,1},{3,0},{4,7},{5,6},{6,5},{7,4},{8,11},{9,10},{10,... | collective-permute-start | bytes 221192 | tf_op jit(solution)/shard_map/ppermute | solution.py:465
  52.8 7.0 %collective-permute-start.16 = (f32[144,128]{1,0:T(8,128)S(1)}, f32[144,128]{1,0:T(8,128)S(1)}, u32[]{:S(2)}, u32[]{:S(2)}) collective-permute-start(f32[144,128]{1,0:T(8,128)S(1)} %add.85), channel_id=1, source_target_pairs={{0,1},{1,0},{2,3},{3,2},{4,5},{5,4},{6,7},{7,6},{8,9},{9,8},{10,11... | collective-permute-start | bytes 221192 | tf_op jit(solution)/shard_map/ppermute | solution.py:465
  59.8 5.3 %collective-permute-start.19 = (f32[192,128]{1,0:T(8,128)S(1)}, f32[192,128]{1,0:T(8,128)S(1)}, u32[]{:S(2)}, u32[]{:S(2)}) collective-permute-start(f32[192,128]{1,0:T(8,128)S(1)} %pad_maximum_fusion.refs_0_), channel_id=1, source_target_pairs={{0,32},{32,0},{64,96},{96,64},{128,160},{160,128},{192,224},{224,1... | collective-permute-start | bytes 294920 | tf_op jit(solution)/shard_map/ppermute | solution.py:315
